TPU v7x, 256 devices: a whole 4x4x8 slice. The times are simulated.
256 devices in a mesh: dp: 16 (over x, y_lo, core), tensor: 16 (over z, y_hi).
Axes of the slice: x: 4, y: 4 (y_hi: 2, y_lo: 2; y = y_hi * 2 + y_lo), z: 8, core: 2. Of those that a mesh axis runs over, the one named last changes fastest.
Arguments:
- tokens: bfloat16 [16, 128, 8192], P('dp', None, 'tensor'), may hold values from -6 to 6
- norm_gain: bfloat16 [8192], P('tensor'), may hold values from 0.5 to 1.5
- w_query: bfloat16 [8192, 4096], P(None, 'tensor'), may hold values from -0.0625 to 0.0625
- w_key: bfloat16 [8192, 512], P(None, 'tensor'), may hold values from -0.0625 to 0.0625
- w_value: bfloat16 [8192, 512], P(None, 'tensor'), may hold values from -0.0625 to 0.0625
- w_output: bfloat16 [4096, 8192], P('tensor'), may hold values from -0.09375 to 0.09375
- positions: int32 [16, 128], P('dp'), may hold values from 0 to 127, as said below
- scale_exps: int32 [7], replicated, may hold values from 2 to 15, as said below
- loss_exp: int32 [1], replicated, may hold values from 12 to 13
- out_grad: bfloat16 [16, 128, 8192], P('dp', None, 'tensor'), may hold values from -6 to 6
Outputs:
- mixed: bfloat16 [16, 128, 8192], P('dp', None, 'tensor')
- d_tokens: bfloat16 [16, 128, 8192], P('dp', None, 'tensor')
- grad_query: float32 [8192, 4096], P('dp', 'tensor')
- grad_key: float32 [8192, 512], P('dp', 'tensor')
- grad_value: float32 [8192, 512], P('dp', 'tensor')
- grad_output: float32 [4096, 8192], P('tensor', 'dp')
Inputs may be any that keep to these rules, and one draw needn't show every extreme that they name: `positions`: in each group the first token's position is 0 and every other token's position is 0 or the previous token's plus one. `scale_exps`: entries belong in order to the casts of normed, w_query, w_key, w_value, w_output, attended and the output gradient; entry 0 is 7 or 8, entries 1 to 4 are 14 or 15, entry 5 is 8 or 9, entry 6 is 2 or 3.
All inputs are finite; a program needn't handle non-finite values.
Results may differ from a plain program's by a relative error of at most 0.028.
Values may be sent and summed in bfloat16 or wider, within the bound.
A program may use at most 128 MiB of HBM per device.

v0:
```python
import math

import jax
import jax.numpy as jnp
from jax import lax
from jax.sharding import PartitionSpec as P

HD = 128
HEADS = 32
KV_HEADS = 4


HIGH = lax.Precision.HIGHEST
E4_TOP = 448.0
E5_TOP = 57344.0


def settle(values):
    return lax.optimization_barrier(values.astype(jnp.bfloat16))


def saturate(values, limit):
    return jnp.clip(values.astype(jnp.float32), -limit, limit)


def rotate(values, positions):
    half = values.shape[-1] // 2
    inverse = jnp.power(500000.0, -2.0 * jnp.arange(half, dtype=jnp.float32) / values.shape[-1])
    angles = positions.astype(jnp.float32)[:, None] * inverse[None, :]
    cosine = jnp.cos(angles)[:, None, :]
    sine = jnp.sin(angles)[:, None, :]
    first = values[..., :half]
    second = values[..., half:]
    return jnp.concatenate(
        [first * cosine - second * sine, second * cosine + first * sine], axis=-1
    )


def probabilities(query, keys, positions):
    count = query.shape[0]
    scores = jnp.einsum(
        "thd,shd->hts", rotate(query, positions), rotate(keys, positions), precision=HIGH
    ) / math.sqrt(query.shape[-1])
    places = jnp.arange(count, dtype=jnp.int32)
    allowed = (places[None, :] <= places[:, None]) & (
        places[None, :] >= places[:, None] - positions[:, None]
    )
    weights = jnp.where(allowed[None], jnp.exp(jnp.where(allowed[None], scores, 0.0)), 0.0)
    return weights / jnp.sum(weights, axis=-1, keepdims=True)


def attention_core(query, keys, values, positions):
    return jnp.einsum("hts,shd->thd", probabilities(query, keys, positions), values, precision=HIGH)


def gather_cols(rows):
    return lax.all_gather(rows, "tensor", axis=1, tiled=True)


def share_cols(term):
    return lax.psum_scatter(
        term.astype(jnp.bfloat16), "tensor", scatter_dimension=1, tiled=True
    ).astype(jnp.float32)


def contract_rows(left, right):
    return lax.dot_general(
        left, right, (((0,), (0,)), ((), ())), preferred_element_type=jnp.float32
    )


def contract_cols(left, right):
    return lax.dot_general(
        left, right, (((1,), (1,)), ((), ())), preferred_element_type=jnp.float32
    )


def body(
    tokens, norm_gain, w_query, w_key, w_value, w_output, positions, scale_exps, loss_exp, out_grad
):
    limits = E4_TOP * jnp.exp2(-scale_exps.astype(jnp.float32))
    grad_top = E5_TOP * jnp.exp2(-(scale_exps[6] + loss_exp[0]).astype(jnp.float32))
    query_cast = saturate(w_query, limits[1]).astype(jnp.bfloat16)
    key_cast = saturate(w_key, limits[2]).astype(jnp.bfloat16)
    value_cast = saturate(w_value, limits[3]).astype(jnp.bfloat16)
    output_cast = saturate(w_output, limits[4]).astype(jnp.bfloat16)
    local_rows = tokens[0].astype(jnp.float32)
    gain_slice = norm_gain.astype(jnp.float32)
    dwidth = local_rows.shape[1] * lax.axis_size("tensor")
    squares = lax.psum(jnp.sum(local_rows * local_rows, axis=1), "tensor")
    inverse_rms = lax.rsqrt(squares / dwidth + 1e-05)
    normed = local_rows * inverse_rms[:, None] * gain_slice[None, :]
    acts = gather_cols(saturate(normed, limits[0]).astype(jnp.bfloat16))
    count = acts.shape[0]
    place = positions[0]
    query = jnp.dot(acts, query_cast, preferred_element_type=jnp.float32).astype(jnp.bfloat16)
    key_cols = jnp.dot(acts, key_cast, preferred_element_type=jnp.float32).astype(jnp.bfloat16)
    value_cols = jnp.dot(acts, value_cast, preferred_element_type=jnp.float32).astype(jnp.bfloat16)
    keys_all, values_all = (
        lax.all_gather(key_cols, "tensor", axis=1, tiled=True),
        lax.all_gather(value_cols, "tensor", axis=1, tiled=True),
    )
    local_heads = query.shape[1] // HD
    head_ids = lax.axis_index("tensor") * local_heads + jnp.arange(local_heads, dtype=jnp.int32)
    kv_ids = head_ids // (HEADS // KV_HEADS)
    selector = (kv_ids[:, None] == jnp.arange(KV_HEADS, dtype=jnp.int32)[None, :]).astype(
        jnp.float32
    )
    query_h = query.astype(jnp.float32).reshape(count, local_heads, HD)
    keys_h = jnp.einsum(
        "tdk,hk->thd",
        keys_all.astype(jnp.float32).reshape(count, HD, KV_HEADS),
        selector,
        precision=HIGH,
    )
    values_h = jnp.einsum(
        "tdk,hk->thd",
        values_all.astype(jnp.float32).reshape(count, HD, KV_HEADS),
        selector,
        precision=HIGH,
    )
    weights = settle(probabilities(query_h, keys_h, place)).astype(jnp.float32)
    attended = (
        jnp.einsum("hts,shd->thd", weights, values_h, precision=HIGH)
        .reshape(count, -1)
        .astype(jnp.bfloat16)
    )
    attended = saturate(attended, limits[5]).astype(jnp.bfloat16)
    mixed = share_cols(jnp.dot(attended, output_cast, preferred_element_type=jnp.float32)).astype(
        jnp.bfloat16
    )
    grad_cast = gather_cols(saturate(out_grad[0], grad_top).astype(jnp.bfloat16))
    d_att = contract_cols(grad_cast, output_cast).astype(jnp.bfloat16)
    _, pullback = jax.vjp(
        lambda left, middle, right: attention_core(left, middle, right, place),
        query_h,
        keys_h,
        values_h,
    )
    d_query_h, d_keys_h, d_values_h = pullback(
        d_att.astype(jnp.float32).reshape(count, local_heads, HD)
    )
    d_query = d_query_h.reshape(count, -1).astype(jnp.bfloat16)
    d_keys_full = jnp.einsum("thd,hk->tdk", d_keys_h, selector, precision=HIGH).reshape(count, -1)
    d_values_full = jnp.einsum("thd,hk->tdk", d_values_h, selector, precision=HIGH).reshape(
        count, -1
    )
    key_sums, value_sums = (
        lax.psum_scatter(
            d_keys_full.astype(jnp.bfloat16), "tensor", scatter_dimension=1, tiled=True
        ).astype(jnp.float32),
        lax.psum_scatter(
            d_values_full.astype(jnp.bfloat16), "tensor", scatter_dimension=1, tiled=True
        ).astype(jnp.float32),
    )
    d_key_cols = key_sums.astype(jnp.bfloat16)
    d_value_cols = value_sums.astype(jnp.bfloat16)
    partial_value = (
        contract_cols(d_query, query_cast)
        + contract_cols(d_key_cols, key_cast)
        + contract_cols(d_value_cols, value_cast)
    )
    d_normed = share_cols(partial_value)
    scaled_grad = gain_slice[None, :] * d_normed
    projection_sum = lax.psum(jnp.sum(local_rows * scaled_grad, axis=1), "tensor")
    cubed = inverse_rms * inverse_rms * inverse_rms
    d_rows = (
        inverse_rms[:, None] * scaled_grad - local_rows * (cubed * projection_sum / dwidth)[:, None]
    ).astype(jnp.bfloat16)
    grad_query, grad_key, grad_value, grad_output = (
        lax.psum_scatter(
            contract_rows(acts, d_query).astype(jnp.bfloat16), "dp", scatter_dimension=0, tiled=True
        ).astype(jnp.float32),
        lax.psum_scatter(
            contract_rows(acts, d_key_cols).astype(jnp.bfloat16),
            "dp",
            scatter_dimension=0,
            tiled=True,
        ).astype(jnp.float32),
        lax.psum_scatter(
            contract_rows(acts, d_value_cols).astype(jnp.bfloat16),
            "dp",
            scatter_dimension=0,
            tiled=True,
        ).astype(jnp.float32),
        lax.psum_scatter(
            contract_rows(attended, grad_cast).astype(jnp.bfloat16),
            "dp",
            scatter_dimension=1,
            tiled=True,
        ).astype(jnp.float32),
    )
    return (mixed[None], d_rows[None], grad_query, grad_key, grad_value, grad_output)


def solution(mesh):
    placed = (
        P("dp", None, "tensor"),
        P("tensor"),
        P(None, "tensor"),
        P(None, "tensor"),
        P(None, "tensor"),
        P("tensor", None),
        P("dp", None),
        P(),
        P(),
        P("dp", None, "tensor"),
    )
    return jax.shard_map(
        body,
        mesh=mesh,
        in_specs=placed,
        out_specs=(
            P("dp", None, "tensor"),
            P("dp", None, "tensor"),
            P("dp", "tensor"),
            P("dp", "tensor"),
            P("dp", "tensor"),
            P("tensor", "dp"),
        ),
        check_vma=False,
    )
```

profile of v0, /device:TPU:6, one launch (start us, length us, event | category | flops | bytes accessed | tf_op | source)
XLA Modules:
  0.0 1388.6 jit_solution(1241107309529312543)
XLA Ops:
  15.2 45.1 %psum.14 = f32[128]{0:T(128)S(1)} all-reduce(f32[128]{0:T(128)S(1)} %fusion.17), channel_id=1, replica_groups=mesh['dp'=16,'tensor'=16] {'tensor'}, use_global_device_ids=true, to_apply=%region_1.2 | all-reduce | flops 128 | bytes 1024 | tf_op jit(solution)/shard_map/psum | solution.py:90
  60.8 2.3 fusion.21
  68.1 31.6 %all-gather.6.cloned.1.call-done = bf16[1,128,8192]{2,1,0:T(8,128)(2,1)} async-done(((bf16[1,128,512]{2,1,0:T(8,128)(2,1)}), bf16[1,128,8192]{2,1,0:T(8,128)(2,1)}) %all-gather.6.cloned.1.call-update) | async-done | bytes 2097168 | tf_op jit(solution)/shard_map/all_gather | solution.py:57
  99.7 5.0 fusion.8
  105.4 79.0 %all-gather.4.cloned.1.call-done = bf16[128,8192]{1,0:T(8,128)(2,1)} async-done(((bf16[128,512]{1,0:T(8,128)(2,1)}), bf16[128,8192]{1,0:T(8,128)(2,1)}) %all-gather.4.cloned.1.call-update) | async-done | bytes 2097168 | tf_op jit(solution)/shard_map/all_gather | solution.py:57
  184.4 3.1 convolution_convert_fusion.9
  187.5 39.1 %all_gather.13 = bf16[128,512]{0,1:T(8,128)(2,1)S(1)} all-gather(bf16[128,32]{0,1:T(8,128)(2,1)S(1)} %convolution_convert_fusion.9), channel_id=1, replica_groups=mesh['dp'=16,'tensor'=16] {'tensor'}, dimensions={1}, use_global_device_ids=true | all-gather | bytes 139264 | tf_op jit(solution)/shard_map/all_gather | solution.py:101
  226.7 3.1 convolution_convert_fusion.8
  229.8 37.2 %all_gather.14 = bf16[128,512]{0,1:T(8,128)(2,1)S(1)} all-gather(bf16[128,32]{0,1:T(8,128)(2,1)S(1)} %convolution_convert_fusion.8), channel_id=1, replica_groups=mesh['dp'=16,'tensor'=16] {'tensor'}, dimensions={1}, use_global_device_ids=true | all-gather | bytes 139264 | tf_op jit(solution)/shard_map/all_gather | solution.py:100
  270.6 4.7 fusion.12
  297.1 190.9 %reduce-scatter.11.cloned.1.call-done = bf16[128,32]{0,1:T(8,128)(2,1)} async-done(((bf16[128,512]{0,1:T(8,128)(2,1)}), bf16[128,32]{0,1:T(8,128)(2,1)}) %reduce-scatter.11.cloned.1.call-update) | async-done | bytes 8208 | tf_op jit(solution)/shard_map/reduce_scatter | solution.py:149
  490.2 199.6 %reduce-scatter.13.cloned.1.call-done = bf16[128,32]{0,1:T(8,128)(2,1)} async-done(((bf16[128,512]{0,1:T(8,128)(2,1)}), bf16[128,32]{0,1:T(8,128)(2,1)}) %reduce-scatter.13.cloned.1.call-update) | async-done | bytes 8208 | tf_op jit(solution)/shard_map/reduce_scatter | solution.py:152
  692.0 4.3 fusion.1
  697.8 2.7 fusion
  702.1 4.8 convolution_convert_fusion
  707.0 3.3 convolution_convert_fusion.1
  710.4 5.6 convolution_convert_fusion.2
  716.0 31.2 %reduce-scatter.19.cloned.1.call-done = bf16[512,32]{0,1:T(8,128)(2,1)} async-done(((bf16[8192,32]{0,1:T(8,128)(2,1)}), bf16[512,32]{0,1:T(8,128)(2,1)}) %reduce-scatter.19.cloned.1.call-update) | async-done | bytes 32784 | tf_op jit(solution)/shard_map/reduce_scatter | solution.py:174
  748.7 63.4 %reduce-scatter.21.cloned.1.call-done = bf16[512,32]{0,1:T(8,128)(2,1)} async-done(((bf16[8192,32]{0,1:T(8,128)(2,1)}), bf16[512,32]{0,1:T(8,128)(2,1)}) %reduce-scatter.21.cloned.1.call-update) | async-done | bytes 32784 | tf_op jit(solution)/shard_map/reduce_scatter | solution.py:180
  813.5 215.6 %reduce-scatter.15.cloned.1.call-done = bf16[128,512]{1,0:T(8,128)(2,1)} async-done(((bf16[128,8192]{1,0:T(8,128)(2,1)}), bf16[128,512]{1,0:T(8,128)(2,1)}) %reduce-scatter.15.cloned.1.call-update) | async-done | bytes 131088 | tf_op jit(solution)/shard_map/reduce_scatter | solution.py:61
  1030.2 39.3 %psum.15 = f32[128]{0:T(128)S(1)} all-reduce(f32[128]{0:T(128)S(1)} %fusion.22), channel_id=1, replica_groups=mesh['dp'=16,'tensor'=16] {'tensor'}, use_global_device_ids=true, to_apply=%region_9.10 | all-reduce | flops 128 | bytes 1024 | tf_op jit(solution)/shard_map/psum | solution.py:165
  1071.2 22.4 %reduce-scatter.23.cloned.1.call-done = bf16[256,512]{1,0:T(8,128)(2,1)} async-done(((bf16[256,8192]{1,0:T(8,128)(2,1)}), bf16[256,512]{1,0:T(8,128)(2,1)}) %reduce-scatter.23.cloned.1.call-update) | async-done | bytes 262160 | tf_op jit(solution)/shard_map/reduce_scatter | solution.py:186
  1095.4 69.0 %reduce-scatter.17.cloned.1.call-done = bf16[512,256]{1,0:T(8,128)(2,1)} async-done(((bf16[8192,256]{1,0:T(8,128)(2,1)}), bf16[512,256]{1,0:T(8,128)(2,1)}) %reduce-scatter.17.cloned.1.call-update) | async-done | bytes 262160 | tf_op jit(solution)/shard_map/reduce_scatter | solution.py:171
  1166.1 215.7 %reduce-scatter.9.cloned.1.call-done = bf16[128,512]{1,0:T(8,128)(2,1)} async-done(((bf16[128,8192]{1,0:T(8,128)(2,1)}), bf16[128,512]{1,0:T(8,128)(2,1)}) %reduce-scatter.9.cloned.1.call-update) | async-done | bytes 131088 | tf_op jit(solution)/shard_map/reduce_scatter | solution.py:61
  (106 shorter events, 51.0 us)
Async XLA Ops:
  7.2 92.5 %all-gather.6.cloned.1.call-start = ((), (), s32[]{:S(2)}) async-start(), calls=%async_computation.17 | async-start | bytes 2228224 | tf_op jit(solution)/shard_map/all_gather | solution.py:57
  11.4 172.9 %all-gather.4.cloned.1.call-start = ((), (), s32[]{:S(2)}) async-start(), calls=%async_computation.8 | async-start | bytes 2228224 | tf_op jit(solution)/shard_map/all_gather | solution.py:57
  12.1 92.5 %copy-start.10 = (f32[512]{0:T(512)}, f32[512]{0:T(512)S(1)}, u32[]{:S(2)}) copy-start(f32[512]{0:T(512)S(1)} %convert_element_type.158) | copy-start | bytes 6148
  60.3 44.4 %copy-start.16 = (f32[128]{0:T(128)}, f32[128]{0:T(128)S(1)}, u32[]{:S(2)}) copy-start(f32[128]{0:T(128)S(1)} %psum.14) | copy-start | bytes 1540
  63.1 424.8 %reduce-scatter.11.cloned.1.call-start = ((), (), s32[]{:S(2)}) async-start(), calls=%async_computation.10 | async-start | bytes 139264 | tf_op jit(solution)/shard_map/reduce_scatter | solution.py:149
  68.0 116.3 %copy-start.1 = (bf16[8192,32]{0,1:T(8,128)(2,1)S(1)}, bf16[8192,32]{0,1:T(8,128)(2,1)}, u32[]{:S(2)}) copy-start(bf16[8192,32]{0,1:T(8,128)(2,1)} %param.14) | copy-start | bytes 1572868
  68.1 158.7 %copy-start.3 = (bf16[8192,32]{0,1:T(8,128)(2,1)S(1)}, bf16[8192,32]{0,1:T(8,128)(2,1)}, u32[]{:S(2)}) copy-start(bf16[8192,32]{0,1:T(8,128)(2,1)} %param.13) | copy-start | bytes 1572868
  184.4 86.2 %copy-start = (bf16[128,8192]{1,0:T(8,128)(2,1)S(1)}, bf16[128,8192]{1,0:T(8,128)(2,1)}, u32[]{:S(2)}) copy-start(bf16[128,8192]{1,0:T(8,128)(2,1)} %all-gather.4.cloned.1.call-done) | copy-start | bytes 6291460
  286.1 203.9 %copy-start.4 = (f32[128,2,64]{2,1,0:T(2,128)S(1)}, f32[128,2,64]{2,1,0:T(2,128)}, u32[]{:S(2)}) copy-start(f32[128,2,64]{2,1,0:T(2,128)} %get-tuple-element.16) | copy-start | bytes 196612
  286.1 203.9 %copy-start.5 = (f32[128,2,64]{2,1,0:T(2,128)S(1)}, f32[128,2,64]{2,1,0:T(2,128)}, u32[]{:S(2)}) copy-start(f32[128,2,64]{2,1,0:T(2,128)} %get-tuple-element.17) | copy-start | bytes 196612
  289.7 400.0 %reduce-scatter.13.cloned.1.call-start = ((), (), s32[]{:S(2)}) async-start(), calls=%async_computation.11 | async-start | bytes 139264 | tf_op jit(solution)/shard_map/reduce_scatter | solution.py:152
  297.1 450.2 %reduce-scatter.19.cloned.1.call-start = ((), (), s32[]{:S(2)}) async-start(), calls=%async_computation.14 | async-start | bytes 557056 | tf_op jit(solution)/shard_map/reduce_scatter | solution.py:174
  489.9 322.2 %reduce-scatter.21.cloned.1.call-start = ((), (), s32[]{:S(2)}) async-start(), calls=%async_computation.15 | async-start | bytes 557056 | tf_op jit(solution)/shard_map/reduce_scatter | solution.py:180
  691.7 337.4 %reduce-scatter.15.cloned.1.call-start = ((), (), s32[]{:S(2)}) async-start(), calls=%async_computation.12 | async-start | bytes 2228224 | tf_op jit(solution)/shard_map/reduce_scatter | solution.py:61
  691.9 4.4 copy-start.12
  697.8 3.4 copy-start.7
  697.8 3.4 copy-start.8
  700.5 393.0 %reduce-scatter.23.cloned.1.call-start = ((), (), s32[]{:S(2)}) async-start(), calls=%async_computation.16 | async-start | bytes 4456448 | tf_op jit(solution)/shard_map/reduce_scatter | solution.py:186
  706.9 457.4 %reduce-scatter.17.cloned.1.call-start = ((), (), s32[]{:S(2)}) async-start(), calls=%async_computation.13 | async-start | bytes 4456448 | tf_op jit(solution)/shard_map/reduce_scatter | solution.py:171
  710.3 318.9 %copy-start.2 = (bf16[1,128,512]{2,1,0:T(8,128)(2,1)S(1)}, bf16[1,128,512]{2,1,0:T(8,128)(2,1)}, u32[]{:S(2)}) copy-start(bf16[1,128,512]{2,1,0:T(8,128)(2,1)} %param.10) | copy-start | bytes 393220
  710.3 318.9 %copy-start.11 = (f32[512]{0:T(512)S(1)}, f32[512]{0:T(512)}, u32[]{:S(2)}) copy-start(f32[512]{0:T(512)} %copy-done.10) | copy-start | bytes 6148
  710.3 359.2 %copy-start.17 = (f32[128]{0:T(128)S(1)}, f32[128]{0:T(128)}, u32[]{:S(2)}) copy-start(f32[128]{0:T(128)} %copy-done.16) | copy-start | bytes 1540
  710.3 359.2 %copy-start.15 = (f32[128]{0:T(128)S(1)}, f32[128]{0:T(128)}, u32[]{:S(2)}) copy-start(f32[128]{0:T(128)} %copy-done.14) | copy-start | bytes 1540
  710.3 671.5 %reduce-scatter.9.cloned.1.call-start = ((), (), s32[]{:S(2)}) async-start(), calls=%async_computation.9 | async-start | bytes 2228224 | tf_op jit(solution)/shard_map/reduce_scatter | solution.py:61
  (4 other events, 7.6 us)
Sparse Core Ops, SparseCore 0:
  11.5 88.0 all-gather.5
  102.7 81.6 all-gather.3
  289.9 198.0 reduce-scatter.10
  492.1 197.6 reduce-scatter.12
  692.7 54.5 reduce-scatter.18
  750.3 61.7 reduce-scatter.20
  816.0 213.0 reduce-scatter.14
  1031.7 61.8 reduce-scatter.22
  1096.1 68.1 reduce-scatter.16
  1168.7 213.0 reduce-scatter.8
where the time goes:
time: 1390 us
  waiting for transfers between devices  1120 us (81%)
  blocking collectives  161 us (12%)
  matrix products  55.5 us (4%)
  other arithmetic  20.3 us (1%)
  between operations  19.7 us (1%)
    reduce_scatter x2, waiting for transfers between devices, share_cols(): lax.psum_scatter(term.astype(jnp.bfloat16), 'tensor', scatter_dimension=1...  431 us
    reduce_scatter x1, waiting for transfers between devices, body(): lax.psum_scatter(d_values_full.astype(jnp.bfloat16), 'tensor', scatter_di...  200 us
    reduce_scatter x1, waiting for transfers between devices, body(): lax.psum_scatter(d_keys_full.astype(jnp.bfloat16), 'tensor', scatter_dime...  191 us
    all_gather x2, waiting for transfers between devices, gather_cols(): return lax.all_gather(rows, 'tensor', axis=1, tiled=True)  111 us
    reduce_scatter x1, waiting for transfers between devices, body(): lax.psum_scatter(contract_rows(acts, d_query).astype(jnp.bfloat16), 'dp',...  69 us
    reduce_scatter x1, waiting for transfers between devices, body(): lax.psum_scatter(contract_rows(acts, d_value_cols).astype(jnp.bfloat16),...  63.4 us
    psum x1, blocking collectives, body(): squares = lax.psum(jnp.sum(local_rows * local_rows, axis=1), 'tensor')  45.1 us
    psum x1, blocking collectives, body(): lax.psum(jnp.sum(local_rows * scaled_grad, axis=1), 'tensor')  39.3 us
  transfers between devices with their start and end apart: 10, of which 10 were waited for; matrix products, arithmetic and copies ran while one was open for 4% of the time, Pallas kernels for 0%

commit v1 on v0

v1 whole, which is shorter than its diff:
```python
import functools
import math

import jax
import jax.numpy as jnp
from jax import lax
from jax.experimental import pallas as pl
from jax.experimental.pallas import tpu as pltpu
from jax.sharding import PartitionSpec as P

HD = 128
E4_TOP = 448.0
E5_TOP = 57344.0
BF = jnp.bfloat16
F32 = jnp.float32
MESH = pl.DeviceIdType.MESH
NZ, NX, TOK, FEAT, QC, KC = 8, 4, 128, 512, 256, 32
DIRS = (1, -1)


def nn(a, b):
    return jnp.dot(a, b, preferred_element_type=F32)


def nt(a, b):
    return lax.dot_general(a, b, (((1,), (1,)), ((), ())), preferred_element_type=F32)


def halves(a):
    high = a.astype(BF)
    return high, (a - high.astype(F32)).astype(BF)


def precise(dot, a, b):
    ah, al = halves(a)
    bh, bl = halves(b)
    return dot(ah, bh) + (dot(ah, bl) + dot(al, bh))


def power_of_half(e):
    out = jnp.float32(1.0)
    for bit in range(5):
        out = out * jnp.where(((e >> bit) & 1) == 1, jnp.float32(2.0 ** -(1 << bit)), jnp.float32(1.0))
    return out


def clip(v, limit):
    return jnp.minimum(jnp.maximum(v, -limit), limit)


def rot(v, c, s):
    return jnp.concatenate([v[:64] * c - v[64:] * s, v[64:] * c + v[:64] * s], axis=0)


def unrot(v, c, s):
    return jnp.concatenate([v[:64] * c + v[64:] * s, v[64:] * c - v[:64] * s], axis=0)


def kernel(
    scale_ref, loss_ref, tok_ref, gain_ref, pos_ref, og_ref, wq_hbm, wk_hbm, wv_hbm, wo_hbm,
    mixed_ref, dtok_ref, gqkv_ref, go_ref,
    wq, wk, wv, wo, acts, gout, pacts, pgout,
    pm, rm, ym, pd, rd, yd,
    sgo, xgo, ygo, sgq, xgq, ygq,
    att_own, att_far, dq_own, dq_far,
    sq, kvs, kvr, dks, dkr, pr,
    qacc, kacc, vacc, dacc,
    load_sem, ga_s, ga_r, gg_s, gg_r, zm_s, zm_r, zd_s, zd_r, xo_s, xo_r, xq_s, xq_r,
    sm_s, sm_r, cp_s, cp_r,
):
    dp = lax.axis_index("dp")
    me = lax.axis_index("tensor")
    z, yh = me // 2, lax.rem(me, 2)
    x, yl, core = dp // 4, lax.rem(dp // 2, 2), lax.rem(dp, 2)
    sent = []

    def copy(src, dst, ssem, rsem, **where):
        return pltpu.make_async_remote_copy(
            src_ref=src, dst_ref=dst, send_sem=ssem, recv_sem=rsem,
            device_id=where, device_id_type=MESH,
        )

    def push(*args, **where):
        c = copy(*args, **where)
        c.start()
        sent.append(c)

    def zdev(sign):
        return lax.rem(z + sign + NZ, NZ) * 2 + yh

    def xdev(sign):
        return lax.rem(x + sign + NX, NX) * 4 + yl * 2 + core

    ypart = z * 2 + (1 - yh)
    ylpart = x * 4 + (1 - yl) * 2 + core
    cpart = x * 4 + yl * 2 + (1 - core)

    loads = [
        pltpu.make_async_copy(wk_hbm, wk, load_sem.at[0]),
        pltpu.make_async_copy(wv_hbm, wv, load_sem.at[1]),
        pltpu.make_async_copy(wq_hbm, wq, load_sem.at[2]),
        pltpu.make_async_copy(wo_hbm, wo, load_sem.at[3]),
    ]
    for c in loads:
        c.start()

    barrier = pltpu.get_barrier_semaphore()

    def greet(o, carry):
        pl.semaphore_signal(
            barrier, inc=1, device_id={"tensor": lax.rem(me + o, 16)}, device_id_type=MESH
        )
        return carry

    lax.fori_loop(1, 16, greet, 0)
    for d in (xdev(1), xdev(-1), ylpart, cpart):
        pl.semaphore_signal(barrier, inc=1, device_id={"dp": d}, device_id_type=MESH)

    lims = [E4_TOP * power_of_half(scale_ref[i]) for i in range(6)]
    glim = E5_TOP * power_of_half(scale_ref[6] + loss_ref[0])

    gout[z, yh] = clip(og_ref[0].astype(F32), glim).astype(BF)
    rows = tok_ref[0].astype(F32)

    def as_row(column):
        return jnp.broadcast_to(column, (TOK, 128)).T

    sq[me] = as_row(jnp.sum(rows * rows, axis=1, keepdims=True))[:8]
    pl.semaphore_wait(barrier, 19)

    def gather(buf, ss, rs):
        def view(zz, k, d, sign):
            v = buf.at[lax.rem(zz + NZ, NZ), yh if k == 0 else 1 - yh]
            if d == 4:
                v = v.at[pl.ds(0 if sign > 0 else TOK // 2, TOK // 2)]
            return v

        def number(d, k, sign):
            return 1 + (d - 1) * 4 + k * 2 + (0 if sign > 0 else 1)

        def side():
            push(buf.at[z, yh], buf.at[z, yh], ss.at[0], rs.at[0], tensor=ypart)

        def wait_side():
            v = buf.at[z, 1 - yh]
            copy(v, v, ss.at[0], rs.at[0], tensor=ypart).wait_recv()

        def send(d, k, sign):
            v = view(z - sign * (d - 1), k, d, sign)
            i = number(d, k, sign)
            push(v, v, ss.at[i], rs.at[i], tensor=zdev(sign))

        def wait(d, k, sign):
            v = view(z - sign * d, k, d, sign)
            i = number(d, k, sign)
            copy(v, v, ss.at[i], rs.at[i], tensor=zdev(sign)).wait_recv()

        return side, wait_side, send, wait

    def exchange(src, dst, j):
        def start(o, carry):
            peer = lax.rem(me + o, 16)
            copy(src(peer), dst.at[me], sm_s.at[j, o], sm_r.at[j, o], tensor=peer).start()
            return carry

        def recv(o, carry):
            origin = lax.rem(me + 16 - o, 16)
            copy(src(me), dst.at[origin], sm_s.at[j, o], sm_r.at[j, o], tensor=origin).wait_recv()
            return carry

        def drain(o, carry):
            peer = lax.rem(me + o, 16)
            copy(src(peer), dst.at[me], sm_s.at[j, o], sm_r.at[j, o], tensor=peer).wait_send()
            return carry

        return (
            lambda: lax.fori_loop(1, 16, start, 0),
            lambda: lax.fori_loop(1, 16, recv, 0),
            lambda: lax.fori_loop(1, 16, drain, 0),
        )

    sq_start, sq_wait, sq_drain = exchange(lambda peer: sq.at[me], sq, 0)
    kv_start, kv_wait, kv_drain = exchange(lambda peer: kvs.at[peer // 4], kvr, 1)
    dk_start, dk_wait, dk_drain = exchange(lambda peer: dks.at[peer], dkr, 2)
    pr_start, pr_wait, pr_drain = exchange(lambda peer: pr.at[me], pr, 3)

    sq_start()
    g_side, g_wait_side, g_send, g_wait = gather(gout, gg_s, gg_r)
    a_side, a_wait_side, a_send, a_wait = gather(acts, ga_s, ga_r)
    g_side()
    for sign in DIRS:
        g_send(1, 0, sign)

    pos = pos_ref[...]
    pair = lax.broadcasted_iota(jnp.int32, (64, TOK), 0).astype(F32)
    angle = pos.astype(F32) * jnp.exp(pair * (-2.0 * math.log(500000.0) / HD))
    cosine, sine = jnp.cos(angle), jnp.sin(angle)

    g_wait_side()
    for sign in DIRS:
        g_send(1, 1, sign)
    sq_wait()
    inv_row = lax.rsqrt(jnp.sum(sq[...], axis=0) / (FEAT * 16) + 1e-05)
    inv = jnp.broadcast_to(inv_row[:1], (128, TOK)).T[:, :1]
    gain = gain_ref[...]
    acts[z, yh] = clip(rows * inv * gain, lims[0]).astype(BF)
    a_side()
    for sign in DIRS:
        a_send(1, 0, sign)

    loads[0].wait()
    loads[1].wait()
    loads[2].wait()

    def trim_in(i, carry):
        r = pl.ds(pl.multiple_of(i * 512, 512), 512)
        wq[r, :] = clip(wq[r, :].astype(F32), lims[1]).astype(BF)
        wk[r, :] = clip(wk[r, :].astype(F32), lims[2]).astype(BF)
        wv[r, :] = clip(wv[r, :].astype(F32), lims[3]).astype(BF)
        return carry

    a_wait_side()
    for sign in DIRS:
        a_send(1, 1, sign)
    lax.fori_loop(0, 16, trim_in, 0)
    qacc[...] = jnp.zeros_like(qacc)
    kacc[...] = jnp.zeros_like(kacc)
    vacc[...] = jnp.zeros_like(vacc)
    dacc[...] = jnp.zeros_like(dacc)

    def project(zz, k):
        zs, ys = lax.rem(zz + NZ, NZ), (yh if k == 0 else 1 - yh)
        r = pl.ds(pl.multiple_of((zs * 2 + ys) * 512, 512), 512)
        a = acts[zs, ys]
        qacc[...] += nn(a, wq[r, :])
        kacc[...] += nn(a, wk[r, :])
        vacc[...] += nn(a, wv[r, :])

    def back(zz, k):
        zs, ys = lax.rem(zz + NZ, NZ), (yh if k == 0 else 1 - yh)
        r = pl.ds(pl.multiple_of((zs * 2 + ys) * 512, 512), 512)
        dacc[...] += nt(wo[:, r], gout[zs, ys])

    for k in (0, 1):
        project(z, k)
    for d in (1, 2, 3):
        for k in (0, 1):
            for sign in DIRS:
                a_wait(d, k, sign)
                a_send(d + 1, k, sign)
        if d == 3:
            for k in (0, 1):
                for sign in DIRS:
                    g_wait(1, k, sign)
                    g_send(2, k, sign)
        for k in (0, 1):
            for sign in DIRS:
                project(z - sign * d, k)

    loads[3].wait()

    def trim_out(i, carry):
        r = pl.ds(pl.multiple_of(i * 512, 512), 512)
        wo[:, r] = clip(wo[:, r].astype(F32), lims[4]).astype(BF)
        return carry

    lax.fori_loop(0, 16, trim_out, 0)
    for k in (0, 1):
        for sign in DIRS:
            a_wait(4, k, sign)
        project(z + 4, k)
    push(acts.at[:, 1 - core], pacts, cp_s.at[0], cp_r.at[0], dp=cpart)

    o64 = lax.broadcasted_iota(jnp.int32, (64, KC), 0)
    c64 = lax.broadcasted_iota(jnp.int32, (64, KC), 1)
    wanted = (o64 & 7) * 4 + (o64 >> 4)
    is_value = ((o64 >> 3) & 1) == 1
    hit = c64 == wanted
    pick_k = jnp.where(hit & jnp.logical_not(is_value), 1.0, 0.0).astype(BF)
    pick_v = jnp.where(hit & is_value, 1.0, 0.0).astype(BF)
    kv_rows = nt(pick_k, kacc[...].astype(BF)) + nt(pick_v, vacc[...].astype(BF))
    kvs[...] = kv_rows.astype(BF).reshape(4, 16, TOK)
    kv_start()
    kvr[me] = kvs[me // 4]

    q_t = qacc[...].astype(BF).astype(F32).T
    q_rot = [rot(q_t[h * HD : (h + 1) * HD], cosine, sine) for h in range(2)]
    for k in (0, 1):
        for sign in DIRS:
            g_wait(2, k, sign)
            g_send(3, k, sign)
    for d in (1, 2):
        for k in (0, 1):
            for sign in DIRS:
                back(z - sign * d, k)

    kv_wait()
    kv = kvr[...].astype(F32)
    k_t = kv[:, :8].reshape(HD, TOK)
    v_t = kv[:, 8:].reshape(HD, TOK)
    k_rot = rot(k_t, cosine, sine)
    k_rows = k_rot.T
    v_t16 = v_t.astype(BF)
    v_rows = v_t.T.astype(BF)
    src = lax.broadcasted_iota(jnp.int32, (TOK, TOK), 0)
    dst = lax.broadcasted_iota(jnp.int32, (TOK, TOK), 1)
    allowed = (src <= dst) & (src >= dst - pos)
    probs = []
    for h in range(2):
        score = precise(nn, k_rows, q_rot[h]) * (1.0 / math.sqrt(HD))
        weight = jnp.where(allowed, jnp.exp(jnp.where(allowed, score, 0.0)), 0.0)
        p = weight / jnp.sum(weight, axis=0, keepdims=True)
        probs.append(p)
        att = nn(v_t16, p.astype(BF)).astype(BF).astype(F32)
        att_own[pl.ds(h * HD, HD), :] = clip(att, lims[5]).astype(BF)
    push(att_own, att_far, cp_s.at[1], cp_r.at[1], dp=cpart)
    att_rows = att_own[...].astype(F32).T.astype(BF)
    for k in (0, 1):
        for sign in DIRS:
            g_wait(3, k, sign)
            g_send(4, k, sign)

    def scatter(p, r, y, ss, rs):
        rows_n = p.shape[2]
        half = rows_n // 2

        def part(v, sign):
            return v.at[pl.ds(0 if sign > 0 else half, half)]

        def number(st, k, sign):
            return (st - 1) * 4 + k * 2 + (0 if sign > 0 else 1)

        def where(zz, k):
            return lax.rem(zz + NZ, NZ), (yh if k == 0 else 1 - yh)

        def ends(st, k, sign):
            to = r.at[0 if sign > 0 else 1, st - 1, k]
            return part(to, sign) if st == 1 else to

        def send(st, k, sign):
            zs, ys = where(z + sign * (5 - st), k)
            v = p.at[zs, ys]
            if st == 1:
                v = part(v, sign)
            i = number(st, k, sign)
            push(v, ends(st, k, sign), ss.at[i], rs.at[i], tensor=zdev(sign))

        def wait(st, k, sign):
            v = ends(st, k, sign)
            i = number(st, k, sign)
            copy(v, v, ss.at[i], rs.at[i], tensor=zdev(sign)).wait_recv()

        def step(st, k, sign):
            wait(st, k, sign)
            zs, ys = where(z + sign * (4 - st), k)
            j = 0 if sign > 0 else 1
            if st == 1:
                a = pl.ds(0 if sign > 0 else half, half)
            else:
                a = pl.ds(0, rows_n)
            p[zs, ys, a] = (p[zs, ys, a].astype(F32) + r[j, st - 1, k, a].astype(F32)).astype(BF)
            send(st + 1, k, sign)

        def total(k):
            for sign in DIRS:
                wait(4, k, sign)
            ys = yh if k == 0 else 1 - yh
            return p[z, ys].astype(F32) + (r[0, 3, k].astype(F32) + r[1, 3, k].astype(F32))

        def cross():
            p[z, 1 - yh] = total(1).astype(BF)
            push(p.at[z, 1 - yh], y, ss.at[16], rs.at[16], tensor=ypart)

        def finish():
            own = total(0)
            copy(y, y, ss.at[16], rs.at[16], tensor=ypart).wait_recv()
            return own + y[...].astype(F32)

        return send, step, cross, finish

    def group_sum(p, r, y, ss, rs):
        rows_n = p.shape[1]
        half = rows_n // 2

        def where(xx, k):
            return lax.rem(xx + NX, NX) * 2 + (yl if k == 0 else 1 - yl)

        def number(st, k, sign):
            return (st - 1) * 4 + k * 2 + (0 if sign > 0 else 1)

        def ends(st, k, sign):
            to = r.at[0 if sign > 0 else 1, st - 1, k]
            return to.at[pl.ds(0 if sign > 0 else half, half)] if st == 1 else to

        def send(st, k, sign):
            v = p.at[where(x + sign * (3 - st), k)]
            if st == 1:
                v = v.at[pl.ds(0 if sign > 0 else half, half)]
            i = number(st, k, sign)
            push(v, ends(st, k, sign), ss.at[i], rs.at[i], dp=xdev(sign))

        def wait(st, k, sign):
            v = ends(st, k, sign)
            i = number(st, k, sign)
            copy(v, v, ss.at[i], rs.at[i], dp=xdev(sign)).wait_recv()

        def step(k, sign):
            wait(1, k, sign)
            s = where(x + sign, k)
            a = pl.ds(0 if sign > 0 else half, half)
            j = 0 if sign > 0 else 1
            p[s, a] = (p[s, a].astype(F32) + r[j, 0, k, a].astype(F32)).astype(BF)
            send(2, k, sign)

        def total(k):
            for sign in DIRS:
                wait(2, k, sign)
            return p[where(x, k)].astype(F32) + (r[0, 1, k].astype(F32) + r[1, 1, k].astype(F32))

        def cross():
            p[where(x, 1)] = total(1).astype(BF)
            push(p.at[where(x, 1)], y, ss.at[8], rs.at[8], dp=ylpart)

        def finish():
            own = total(0)
            copy(y, y, ss.at[8], rs.at[8], dp=ylpart).wait_recv()
            return own + y[...].astype(F32)

        return send, step, cross, finish

    m_send, m_step, m_cross, m_finish = scatter(pm, rm, ym, zm_s, zm_r)
    n_send, n_step, n_cross, n_finish = scatter(pd, rd, yd, zd_s, zd_r)
    o_send, o_step, o_cross, o_finish = group_sum(sgo, xgo, ygo, xo_s, xo_r)
    w_send, w_step, w_cross, w_finish = group_sum(sgq, xgq, ygq, xq_s, xq_r)
    K_ORDER = (1, 0)

    def mix(i, carry):
        zs, ys = lax.rem(z + 4 + i // 2, NZ), lax.rem(i, 2)
        r = pl.ds(pl.multiple_of((zs * 2 + ys) * 512, 512), 512)
        pm[zs, ys] = nn(att_rows, wo[:, r]).astype(BF)
        return carry

    lax.fori_loop(0, 2, mix, 0)
    for k in K_ORDER:
        for sign in DIRS:
            m_send(1, k, sign)
    lax.fori_loop(2, 16, mix, 0)

    for k in (0, 1):
        for sign in DIRS:
            g_wait(4, k, sign)
    push(gout.at[:, 1 - core], pgout, cp_s.at[2], cp_r.at[2], dp=cpart)
    for k in (0, 1):
        for sign in DIRS:
            m_step(1, 1 - k, sign)
    for k in (0, 1):
        back(z, k)
        back(z + 4, k)
        for sign in DIRS:
            back(z - sign * 3, k)

    d_t = dacc[...].astype(BF)
    dk_rot = jnp.zeros((HD, TOK), F32)
    dv_t = jnp.zeros((HD, TOK), F32)
    for h in range(2):
        g = d_t[h * HD : (h + 1) * HD]
        p = probs[h]
        dw = nn(v_rows, g)
        delta = jnp.sum(p * dw, axis=0, keepdims=True)
        ds = p * (dw - delta) * (1.0 / math.sqrt(HD))
        p_high, p_low = halves(p)
        dv_t = dv_t + nt(g, p_high) + nt(g, p_low)
        dq_own[pl.ds(h * HD, HD), :] = unrot(precise(nn, k_rot, ds), cosine, sine).astype(BF)
        dk_rot = dk_rot + precise(nt, q_rot[h], ds)
    dk_t = unrot(dk_rot, cosine, sine)
    dks[...] = jnp.concatenate(
        [dk_t.reshape(16, 8, TOK), dv_t.reshape(16, 8, TOK)], axis=1
    ).astype(BF)
    dk_start()
    dkr[me] = dks[me]

    copy(gout.at[:, core], pgout, cp_s.at[2], cp_r.at[2], dp=cpart).wait_recv()
    copy(att_own, att_far, cp_s.at[1], cp_r.at[1], dp=cpart).wait_recv()

    def out_grads(i, carry):
        s = lax.rem(2 * x + 4 + i, 8)
        sgo[s] = (nn(att_own[...], gout[s, core]) + nn(att_far[...], pgout[s])).astype(BF)
        return carry

    lax.fori_loop(0, 2, out_grads, 0)
    for k in K_ORDER:
        for sign in DIRS:
            o_send(1, k, sign)
    lax.fori_loop(2, 8, out_grads, 0)
    for k in K_ORDER:
        for sign in DIRS:
            m_step(2, k, sign)

    dk_wait()
    o4 = lax.broadcasted_iota(jnp.int32, (64, 64), 0)
    i4 = lax.broadcasted_iota(jnp.int32, (64, 64), 1)
    low = o4 & 31
    pick = jnp.where(i4 == (low & 3) * 16 + (o4 >> 5) * 8 + (low >> 2), 1.0, 0.0).astype(BF)
    dkv = jnp.sum(dkr[...].astype(F32).reshape(4, 4, 16, TOK), axis=1).reshape(64, TOK)
    dq_own[pl.ds(QC, 64), :] = nn(pick, dkv.astype(BF)).astype(BF)
    push(dq_own, dq_far, cp_s.at[3], cp_r.at[3], dp=cpart)

    def down(i, carry):
        zs, ys = lax.rem(z + 4 + i // 2, NZ), lax.rem(i, 2)
        r = pl.ds(pl.multiple_of((zs * 2 + ys) * 512, 512), 512)
        term = nn(wq[r, :], dq_own[pl.ds(0, QC), :])
        term = term + nn(wk[r, :], dq_own[pl.ds(QC, KC), :])
        term = term + nn(wv[r, :], dq_own[pl.ds(QC + KC, KC), :])
        pd[zs, ys] = term.astype(BF)
        return carry

    lax.fori_loop(0, 2, down, 0)
    for k in K_ORDER:
        for sign in DIRS:
            m_step(3, k, sign)
    for k in K_ORDER:
        for sign in DIRS:
            n_send(1, k, sign)
    lax.fori_loop(2, 16, down, 0)
    for k in K_ORDER:
        for sign in DIRS:
            o_step(k, sign)

    copy(acts.at[:, core], pacts, cp_s.at[0], cp_r.at[0], dp=cpart).wait_recv()
    copy(dq_own, dq_far, cp_s.at[3], cp_r.at[3], dp=cpart).wait_recv()

    def in_grads(i, carry):
        s = lax.rem(2 * x + 4 + i, 8)
        sgq[s] = (nn(dq_own[...], acts[s, core]) + nn(dq_far[...], pacts[s])).astype(BF)
        return carry

    lax.fori_loop(0, 2, in_grads, 0)
    for k in K_ORDER:
        for sign in DIRS:
            w_send(1, k, sign)
    lax.fori_loop(2, 8, in_grads, 0)

    for k in K_ORDER:
        for sign in DIRS:
            n_step(1, k, sign)
    m_cross()
    for k in K_ORDER:
        for sign in DIRS:
            n_step(2, k, sign)
    mixed_ref[0] = m_finish().astype(BF)
    o_cross()
    for k in K_ORDER:
        for sign in DIRS:
            w_step(k, sign)
    for k in K_ORDER:
        for sign in DIRS:
            n_step(3, k, sign)
    go_ref[...] = o_finish()
    n_cross()
    w_cross()
    scaled = n_finish().T * gain
    pr[me] = as_row(jnp.sum(rows * scaled, axis=1, keepdims=True))[:8]
    pr_start()
    gqkv_ref[...] = w_finish()
    pr_wait()
    proj = jnp.broadcast_to(jnp.sum(pr[...], axis=0)[:1], (128, TOK)).T[:, :1]
    slope = inv * inv * inv * proj / (FEAT * 16)
    dtok_ref[0] = (inv * scaled - rows * slope).astype(BF)

    for c in sent:
        c.wait_send()
    sq_drain()
    kv_drain()
    dk_drain()
    pr_drain()


def body(
    tokens, norm_gain, w_query, w_key, w_value, w_output, positions, scale_exps, loss_exp, out_grad
):
    vmem = pl.BlockSpec(memory_space=pltpu.VMEM)
    smem = pl.BlockSpec(memory_space=pltpu.SMEM)
    hbm = pl.BlockSpec(memory_space=pl.ANY)
    V = pltpu.VMEM
    dma = pltpu.SemaphoreType.DMA
    mixed, d_rows, gqkv, grad_output = pl.pallas_call(
        kernel,
        out_shape=(
            jax.ShapeDtypeStruct((1, TOK, FEAT), BF),
            jax.ShapeDtypeStruct((1, TOK, FEAT), BF),
            jax.ShapeDtypeStruct((QC + 2 * KC, FEAT), F32),
            jax.ShapeDtypeStruct((QC, FEAT), F32),
        ),
        in_specs=[smem, smem, vmem, vmem, vmem, vmem, hbm, hbm, hbm, hbm],
        out_specs=(vmem, vmem, vmem, vmem),
        scratch_shapes=[
            V((8192, QC), BF), V((8192, KC), BF), V((8192, KC), BF), V((QC, 8192), BF),
            V((8, 2, TOK, FEAT), BF), V((8, 2, TOK, FEAT), BF),
            V((8, TOK, FEAT), BF), V((8, TOK, FEAT), BF),
            V((8, 2, TOK, FEAT), BF), V((2, 4, 2, TOK, FEAT), BF), V((TOK, FEAT), BF),
            V((8, 2, FEAT, TOK), BF), V((2, 4, 2, FEAT, TOK), BF), V((FEAT, TOK), BF),
            V((8, QC, FEAT), BF), V((2, 2, 2, QC, FEAT), BF), V((QC, FEAT), BF),
            V((8, QC + 64, FEAT), BF), V((2, 2, 2, QC + 64, FEAT), BF), V((QC + 64, FEAT), BF),
            V((QC, TOK), BF), V((QC, TOK), BF), V((QC + 64, TOK), BF), V((QC + 64, TOK), BF),
            V((16, 8, TOK), F32), V((4, 16, TOK), BF), V((16, 16, TOK), BF),
            V((16, 16, TOK), BF), V((16, 16, TOK), BF), V((16, 8, TOK), F32),
            V((TOK, QC), F32), V((TOK, KC), F32), V((TOK, KC), F32), V((QC, TOK), F32),
            dma((4,)), dma((17,)), dma((17,)), dma((17,)), dma((17,)),
            dma((17,)), dma((17,)), dma((17,)), dma((17,)),
            dma((9,)), dma((9,)), dma((9,)), dma((9,)),
            dma((4, 16)), dma((4, 16)), dma((4,)), dma((4,)),
        ],
        compiler_params=pltpu.CompilerParams(
            collective_id=0, has_side_effects=True, vmem_limit_bytes=60 * 1024 * 1024
        ),
    )(
        scale_exps, loss_exp, tokens, norm_gain.astype(F32)[None], positions, out_grad,
        w_query, w_key, w_value, w_output,
    )
    grad_query = gqkv[:QC].T
    grad_key = gqkv[QC : QC + KC].T
    grad_value = gqkv[QC + KC :].T
    return mixed, d_rows, grad_query, grad_key, grad_value, grad_output


def solution(mesh):
    placed = (
        P("dp", None, "tensor"),
        P("tensor"),
        P(None, "tensor"),
        P(None, "tensor"),
        P(None, "tensor"),
        P("tensor", None),
        P("dp", None),
        P(),
        P(),
        P("dp", None, "tensor"),
    )
    return jax.shard_map(
        body,
        mesh=mesh,
        in_specs=placed,
        out_specs=(
            P("dp", None, "tensor"),
            P("dp", None, "tensor"),
            P("dp", "tensor"),
            P("dp", "tensor"),
            P("dp", "tensor"),
            P("tensor", "dp"),
        ),
        check_vma=False,
    )
```

time: 1390 us -> 138 us (0.10)
  waiting for transfers between devices: 1120 us -> 0 us
  blocking collectives: 161 us -> 0 us
  Pallas kernels: 0 us -> 120 us
  matrix products: 55.5 us -> 0 us
  other arithmetic: 20.3 us -> 1.26 us
  between operations: 19.7 us -> 1.29 us
    reduce_scatter x8 -> x0, waiting for transfers between devices: 1010 us -> none  [the longest x2 431 us: share_cols(): lax.psum_scatter(term.astype(jnp.bfloat16), 'tensor', scatter_dimension=1...]
    pallas_call x0 -> x1, Pallas kernels: none -> 120 us  [body(): pl.pallas_call(kernel, out_shape=(jax.ShapeDtypeStruct((1, TOK, FEAT), BF...]
    all_gather x2 -> x0, waiting for transfers between devices: 111 us -> none  [gather_cols(): return lax.all_gather(rows, 'tensor', axis=1, tiled=True)]
    psum x2 -> x0, blocking collectives: 84.4 us -> none  [the longest x1 45.1 us: body(): squares = lax.psum(jnp.sum(local_rows * local_rows, axis=1), 'tensor')]
    all_gather x2 -> x0, blocking collectives: 76.3 us -> none  [the longest x1 39.1 us: body(): lax.all_gather(value_cols, 'tensor', axis=1, tiled=True)]
    dot_general x22 -> x0, matrix products: 55.5 us -> none  [the longest x4 13.4 us: contract_cols(): lax.dot_general(left, right, (((1,), (1,)), ((), ())), preferred_element_...]
  transfers between devices with their start and end apart: 10 -> 0, of which waited for: 10 -> 0; matrix products, arithmetic and copies ran while one was open for 4% -> 0% of each run, Pallas kernels for 0% -> 0%
where the time goes in v1:
time: 138 us; the launch traced here: 136 us
  Pallas kernels  120 us (87%)
  local copies, waits for them, and re-layouts  13.9 us (10%)
    pallas_call x1, Pallas kernels, body(): pl.pallas_call(kernel, out_shape=(jax.ShapeDtypeStruct((1, TOK, FEAT), BF...  120 us
    unnamed x6, local copies, waits for them, and re-layouts  11.3 us

profile of v1, /device:TPU:6, one launch (start us, length us, event | category | flops | bytes accessed | tf_op | source)
XLA Modules:
  0.0 136.3 jit_solution(4957478297870281804)
XLA Ops:
  1.3 1.3 broadcast_in_dim.7
  2.5 2.7 %copy.16.wk_hbm = bf16[8192,32]{1,0:T(8,128)(2,1)} copy(bf16[8192,32]{0,1:T(8,128)(2,1)} %param.13) | data formatting | bytes 1048576 | tf_op args[3]
  5.2 2.6 %copy.17.wv_hbm = bf16[8192,32]{1,0:T(8,128)(2,1)} copy(bf16[8192,32]{0,1:T(8,128)(2,1)} %param.14) | data formatting | bytes 1048576 | tf_op args[4]
  7.8 119.8 %shard_map.145 = (bf16[1,128,512]{2,1,0:T(8,128)(2,1)}, bf16[1,128,512]{2,1,0:T(8,128)(2,1)}, f32[320,512]{1,0:T(8,128)}, f32[256,512]{1,0:T(8,128)}) custom-call(s32[7]{0:T(128)} %scale_ref.1, s32[1]{0:T(128)S(6)} %copy.22.loss_ref, bf16[1,128,512]{2,1,0:T(8,128)(2,1)} %tok_ref.1, f32[1,512]{1,0:T(1,128)} %bitcast.7, s32[1,128]{1,0:T(1,128)} %pos_ref.1, ...), custom_call_target="tpu_custom_call" | custom-call | tf_op jit(solution)/shard_map/pallas_call | solution.py:586
  127.7 1.5 %slice_bitcast_fusion.1 = (f32[512,32]{0,1:T(8,128)}, f32[512,32]{0,1:T(8,128)}) fusion(f32[320,512]{1,0:T(8,128)} %get-tuple-element.12), kind=kLoop, calls=%fused_computation.1 | loop fusion | bytes 262144 | tf_op jit(solution)/shard_map/transpose | solution.py:622
  129.2 1.1 slice_bitcast_fusion
  130.3 1.0 copy.18
  131.3 1.6 %copy.23 = bf16[1,128,512]{2,1,0:T(8,128)(2,1)} copy(bf16[1,128,512]{2,1,0:T(8,128)(2,1)} %get-tuple-element.28) | data formatting | bytes 262144
  132.9 1.6 %copy.24 = bf16[1,128,512]{2,1,0:T(8,128)(2,1)} copy(bf16[1,128,512]{2,1,0:T(8,128)(2,1)} %get-tuple-element.29) | data formatting | bytes 262144
  134.4 1.9 %copy.25 = f32[256,512]{1,0:T(8,128)} copy(f32[256,512]{1,0:T(8,128)} %get-tuple-element.33) | data formatting | bytes 1048576

commit v2 on v0

v2 whole, which is shorter than its diff:
```python
import functools
import math

import jax
import jax.numpy as jnp
from jax import lax
from jax.experimental import pallas as pl
from jax.experimental.pallas import tpu as pltpu
from jax.sharding import PartitionSpec as P

HD = 128
E4_TOP = 448.0
E5_TOP = 57344.0
BF = jnp.bfloat16
F32 = jnp.float32
MESH = pl.DeviceIdType.MESH
NZ, NX, TOK, FEAT, QC, KC = 8, 4, 128, 512, 256, 32
DIRS = (1, -1)


def nn(a, b):
    return jnp.dot(a, b, preferred_element_type=F32)


def nt(a, b):
    return lax.dot_general(a, b, (((1,), (1,)), ((), ())), preferred_element_type=F32)


def halves(a):
    high = a.astype(BF)
    return high, (a - high.astype(F32)).astype(BF)


def precise(dot, a, b):
    ah, al = halves(a)
    bh, bl = halves(b)
    return dot(ah, bh) + (dot(ah, bl) + dot(al, bh))


def power_of_half(e):
    out = jnp.float32(1.0)
    for bit in range(5):
        out = out * jnp.where(((e >> bit) & 1) == 1, jnp.float32(2.0 ** -(1 << bit)), jnp.float32(1.0))
    return out


def clip(v, limit):
    return jnp.minimum(jnp.maximum(v, -limit), limit)


def rot(v, c, s):
    return jnp.concatenate([v[:64] * c - v[64:] * s, v[64:] * c + v[:64] * s], axis=0)


def unrot(v, c, s):
    return jnp.concatenate([v[:64] * c + v[64:] * s, v[64:] * c - v[:64] * s], axis=0)


ORDER = (
    0, 16, 32, 2, 9, 1, 33, 78, 108, 58, 113, 98, 68, 73, 93, 48, 43, 118, 83, 63, 44, 88, 53, 103,
    52, 3, 10, 13, 62, 47, 6, 57, 82, 42, 18, 25, 17, 49, 84, 54, 12, 92, 5, 87, 4, 7, 67, 11, 72,
    14, 19, 26, 64, 59, 22, 29, 21, 28, 94, 89, 97, 102, 107, 8, 15, 77, 112, 20, 27, 23, 69, 30,
    74, 99, 104, 117, 34, 24, 35, 31, 79, 38, 109, 114, 119, 37, 36, 80, 120, 123, 39, 115, 132,
    75, 110, 126, 160, 164, 70, 100, 127, 105, 133, 40, 65, 60, 155, 90, 161, 153, 157, 95, 162,
    156, 124, 163, 154, 55, 171, 177, 175, 179, 128, 45, 134, 85, 169, 166, 165, 50, 41, 121, 138,
    81, 116, 51, 147, 111, 141, 135, 76, 129, 159, 158, 91, 106, 148, 71, 46, 86, 66, 56, 96, 61,
    101, 142, 125, 122, 183, 187, 181, 185, 186, 139, 136, 192, 193, 130, 191, 178, 170, 149, 176,
    143, 180, 167, 168, 184, 190, 194, 172, 150, 144, 131, 137, 188, 189, 140, 199, 151, 145, 182,
    196, 195, 198, 174, 173, 152, 146, 197, 201, 202, 203, 200,
)


def kernel(
    scale_ref, loss_ref, tok_ref, gain_ref, pos_ref, og_ref, wq_hbm, wk_hbm, wv_hbm, wo_hbm,
    mixed_hbm, dtok_hbm, gq_hbm, gkv_hbm, go_hbm,
    mixed_out, dtok_out, gq_out, go_out, gkv_out,
    wq, wkt, wvt, wkv, wo, toks, acts, gout, pacts, pgout,
    pm, rm0, rm1, ym, pd, rd0, rd1, yd,
    sgo, xgo, ygo, sgw, xgw, ygw, sgv, xgv, ygv,
    att_own, att_far, dq_own, dq_far, dk_own, dk_far, probs, q_rot, k_rot, v_rows, lane_inv,
    angles, projected, scaled_rows,
    mg, kvs, kvr, dks, dkr, pr,
    qacc, kvacc, dacc,
    load_sem, out_sem, gt_s, gt_r, gg_s, gg_r, zm_s, zm_r, zd_s, zd_r, xo_s, xo_r,
    xw_s, xw_r, xv_s, xv_r, sm_s, sm_r, cp_s, cp_r,
):
    dp = lax.axis_index("dp")
    me = lax.axis_index("tensor")
    z, yh = me // 2, lax.rem(me, 2)
    x, yl, core = dp // 4, lax.rem(dp // 2, 2), lax.rem(dp, 2)
    sent = []
    tasks = {}
    K_ORDER = (1, 0)
    SLOTS = [(d, k, g) for k in (0, 1) for d in range(5) for g in (DIRS if 0 < d < 4 else (1,))]

    def name(head, *parts):
        return head + ",".join(("+" if v > 0 else "-") if n == len(parts) - 1 else str(v) for n, v in enumerate(parts))

    def task(key, *steps):
        tasks[key] = steps

    def call(f, *args):
        return functools.partial(f, *args)

    def copy(src, dst, ssem, rsem, **where):
        return pltpu.make_async_remote_copy(
            src_ref=src, dst_ref=dst, send_sem=ssem, recv_sem=rsem,
            device_id=where, device_id_type=MESH,
        )

    def push(*args, **where):
        c = copy(*args, **where)
        c.start()
        sent.append(c)

    def zdev(sign):
        return lax.rem(z + sign + NZ, NZ) * 2 + yh

    def xdev(sign):
        return lax.rem(x + sign + NX, NX) * 4 + yl * 2 + core

    ypart = z * 2 + (1 - yh)
    ylpart = x * 4 + (1 - yl) * 2 + core
    cpart = x * 4 + yl * 2 + (1 - core)

    loads = [
        pltpu.make_async_copy(wk_hbm, wkt, load_sem.at[0]),
        pltpu.make_async_copy(wv_hbm, wvt, load_sem.at[1]),
        pltpu.make_async_copy(wq_hbm, wq, load_sem.at[2]),
        pltpu.make_async_copy(wo_hbm, wo, load_sem.at[3]),
    ]
    for c in loads:
        c.start()

    barrier = pltpu.get_barrier_semaphore()

    def greet(o, carry):
        pl.semaphore_signal(
            barrier, inc=1, device_id={"tensor": lax.rem(me + o, 16)}, device_id_type=MESH
        )
        return carry

    lax.fori_loop(1, 16, greet, 0)
    for other in (xdev(1), xdev(-1), ylpart, cpart):
        pl.semaphore_signal(barrier, inc=1, device_id={"dp": other}, device_id_type=MESH)

    lims = [E4_TOP * power_of_half(scale_ref[i]) for i in range(6)]
    glim = E5_TOP * power_of_half(scale_ref[6] + loss_ref[0])

    toks[z, yh] = tok_ref[0]
    gout[z, yh] = clip(og_ref[0].astype(F32), glim).astype(BF)
    rows = tok_ref[0].astype(F32)
    gain = gain_ref[...].astype(F32).reshape(1, FEAT)

    def as_row(column):
        return jnp.broadcast_to(column, (TOK, 128)).T

    lanes = [gain[:, i * 128 : (i + 1) * 128] for i in range(4)]
    squares_own = as_row(jnp.sum(rows * rows, axis=1, keepdims=True))[:4]
    mg[me] = jnp.concatenate(lanes + [squares_own], axis=0)
    pos = pos_ref[...]
    pair = lax.broadcasted_iota(jnp.int32, (64, TOK), 0).astype(F32)
    angle = pos.astype(F32) * jnp.exp(pair * (-2.0 * math.log(500000.0) / HD))
    angles[0] = jnp.cos(angle)
    angles[1] = jnp.sin(angle)
    qacc[...] = jnp.zeros_like(qacc)
    kvacc[...] = jnp.zeros_like(kvacc)
    dacc[...] = jnp.zeros_like(dacc)
    projected[...] = jnp.zeros_like(projected)
    pl.semaphore_wait(barrier, 19)

    def spot(zz, k):
        return lax.rem(zz + NZ, NZ), (yh if k == 0 else 1 - yh)

    def half_of(sign):
        return pl.ds(0 if sign > 0 else TOK // 2, TOK // 2)

    def gather(p, buf, ss, rs):
        def view(zz, k, part=None):
            zs, ys = spot(zz, k)
            return buf.at[zs, ys] if part is None else buf.at[zs, ys, half_of(part)]

        def ring(d, k, sign, zz):
            cut = sign if (d == 4 or (d == 2 and k == 1)) else None
            i = (d - 1) * 2 + (0 if sign > 0 else 1) + 8 * k
            return view(zz, k, cut), i

        def send(d, k, sign):
            v, i = ring(d, k, sign, z - sign * (d - 1))
            push(v, v, ss.at[i], rs.at[i], tensor=zdev(sign))

        def wait(d, k, sign):
            v, i = ring(d, k, sign, z - sign * d)
            copy(v, v, ss.at[i], rs.at[i], tensor=zdev(sign)).wait_recv()

        def side(d, k, sign):
            i = 12 + d * 2 + (0 if sign > 0 else 1)
            cut = {0: None, 2: -sign, 3: None, 4: sign}[d]
            return view(z - sign * d, k, cut), i

        def send_side(d, sign):
            v, i = side(d, 0, sign)
            push(v, v, ss.at[i], rs.at[i], tensor=ypart)

        def wait_side(d, sign):
            v, i = side(d, 1, sign)
            copy(v, v, ss.at[i], rs.at[i], tensor=ypart).wait_recv()

        def begin():
            send_side(0, 1)
            for g in DIRS:
                send(1, 0, g)

        def partner():
            wait_side(0, 1)
            for g in DIRS:
                send(1, 1, g)

        task(p + "0", begin)
        task(p + "f1,1", partner)
        for g in DIRS:
            for d, k in ((2, 0), (3, 0), (4, 0), (2, 1)):
                task(name(p + "f", d, k, g), call(wait, d - 1, k, g), call(send, d, k, g))
            task(name(p + "s2,", g), call(send_side, 2, g))
            task(name(p + "s3,", g), call(send_side, 3, g))
            task(name(p + "s4,", g), call(wait, 4, 0, g), call(send_side, 4, g))

        def arrived(d, k, g):
            if k == 1 and d > 0:
                if d == 1:
                    return
                if d == 2:
                    wait(2, 1, g)
                for h in DIRS if d == 4 else (g,):
                    wait_side(d, h)

        return arrived

    def exchange(src, dst, j):
        def start(o, carry):
            peer = lax.rem(me + o, 16)
            copy(src(peer), dst.at[me], sm_s.at[j, o], sm_r.at[j, o], tensor=peer).start()
            return carry

        def recv(o, carry):
            origin = lax.rem(me + 16 - o, 16)
            copy(src(me), dst.at[origin], sm_s.at[j, o], sm_r.at[j, o], tensor=origin).wait_recv()
            return carry

        def drain(o, carry):
            peer = lax.rem(me + o, 16)
            copy(src(peer), dst.at[me], sm_s.at[j, o], sm_r.at[j, o], tensor=peer).wait_send()
            return carry

        return (
            lambda: lax.fori_loop(1, 16, start, 0),
            lambda: lax.fori_loop(1, 16, recv, 0),
            lambda: lax.fori_loop(1, 16, drain, 0),
        )

    mg_start, mg_wait, mg_drain = exchange(lambda peer: mg.at[me], mg, 0)
    kv_start, kv_wait, kv_drain = exchange(lambda peer: kvs.at[peer // 4], kvr, 1)
    dk_start, dk_wait, dk_drain = exchange(lambda peer: dks.at[peer], dkr, 2)
    pr_start, pr_wait, pr_drain = exchange(lambda peer: pr.at[me], pr, 3)

    t_arrived = gather("T", toks, gt_s, gt_r)
    g_arrived = gather("G", gout, gg_s, gg_r)
    task("mg", mg_start)

    def gain_of(slot):
        g = mg[slot]
        return jnp.concatenate([g[i : i + 1] for i in range(4)], axis=1)

    def prepare():
        mg_wait()
        squares = jnp.sum(mg[...], axis=0)[4:5]
        inv_row = lax.rsqrt(squares / (FEAT * 16) + 1e-05)
        lane_inv[...] = jnp.broadcast_to(inv_row[:1], (128, TOK)).T
        for c in loads:
            c.wait()

    task("pre", prepare)

    def block(d, k, g):
        zs, ys = spot(z - g * d, k)
        return zs, ys, pl.ds(pl.multiple_of((zs * 2 + ys) * 512, 512), 512)

    def project(d, k, g):
        t_arrived(d, k, g)
        zs, ys, r = block(d, k, g)
        inv = lane_inv[:, pl.ds(0, 1)]
        a = toks[zs, ys].astype(F32) * inv * gain_of(zs * 2 + ys)
        a = clip(a, lims[0]).astype(BF)
        acts[zs, ys] = a
        w = clip(wq[r, :].astype(F32), lims[1]).astype(BF)
        wq[r, :] = w
        wn = jnp.concatenate(
            [clip(wkt[:, r].astype(F32), lims[2]), clip(wvt[:, r].astype(F32), lims[3])], axis=0
        ).T.astype(BF)
        wkv[r, :] = wn
        qacc[...] += nn(a, w)
        kvacc[...] += nn(a, wn)

    def cast_out(d, k, g):
        zs, ys, r = block(d, k, g)
        wo[:, r] = clip(wo[:, r].astype(F32), lims[4]).astype(BF)

    def back(d, k, g):
        g_arrived(d, k, g)
        zs, ys, r = block(d, k, g)
        dacc[...] += nt(wo[:, r], gout[zs, ys])

    def natural(i):
        low = i & 31
        return (low & 3) * 16 + (i >> 5) * 8 + (low >> 2)

    i0 = lax.broadcasted_iota(jnp.int32, (64, 64), 0)
    i1 = lax.broadcasted_iota(jnp.int32, (64, 64), 1)

    def send_kv():
        by_head = jnp.where(natural(i1) == i0, 1.0, 0.0).astype(BF)
        kvs[...] = nt(by_head, kvacc[...].astype(BF)).astype(BF).reshape(4, 16, TOK)
        kv_start()
        kvr[me] = kvs[me // 4]

    task("kv", send_kv)

    def turn_query():
        q_t = qacc[...].astype(BF).astype(F32).T
        for h in range(2):
            q_rot[h] = rot(q_t[h * HD : (h + 1) * HD], angles[0], angles[1])

    task("qrot", turn_query)

    def attend():
        kv_wait()
        kv = kvr[...].astype(F32)
        k_t = kv[:, :8].reshape(HD, TOK)
        v_t = kv[:, 8:].reshape(HD, TOK)
        k_turned = rot(k_t, angles[0], angles[1])
        k_rot[...] = k_turned
        k_rows = k_turned.T
        v_t16 = v_t.astype(BF)
        v_rows[...] = v_t.T.astype(BF)
        src = lax.broadcasted_iota(jnp.int32, (TOK, TOK), 0)
        dst = lax.broadcasted_iota(jnp.int32, (TOK, TOK), 1)
        allowed = (src <= dst) & (src >= dst - pos)
        for h in range(2):
            score = precise(nn, k_rows, q_rot[h]) * (1.0 / math.sqrt(HD))
            weight = jnp.where(allowed, jnp.exp(jnp.where(allowed, score, 0.0)), 0.0)
            p = weight / jnp.sum(weight, axis=0, keepdims=True)
            probs[h] = p
            att = nn(v_t16, p.astype(BF)).astype(BF).astype(F32)
            att_own[pl.ds(h * HD, HD), :] = clip(att, lims[5]).astype(BF)
        push(att_own, att_far, cp_s.at[1], cp_r.at[1], dp=cpart)

    task("att", attend)

    def mix(d, k, g):
        zs, ys, r = block(d, k, -g)
        att_rows = att_own[...].astype(F32).T.astype(BF)
        pm[zs, ys] = nn(att_rows, wo[:, r]).astype(BF)

    def share_gout():
        push(gout.at[:, 1 - core], pgout, cp_s.at[2], cp_r.at[2], dp=cpart)

    def share_acts():
        push(acts.at[:, 1 - core], pacts, cp_s.at[0], cp_r.at[0], dp=cpart)

    task("gpush", share_gout)
    task("apush", share_acts)

    def score_grad(h):
        g = dacc[pl.ds(h * HD, HD), :].astype(BF)
        dw = nn(v_rows[...], g)
        p = probs[h]
        delta = jnp.sum(p * dw, axis=0, keepdims=True)
        return g, p, p * (dw - delta) * (1.0 / math.sqrt(HD))

    def backward():
        dk_rot = jnp.zeros((HD, TOK), F32)
        dv_t = jnp.zeros((HD, TOK), F32)
        for h in range(2):
            g, p, ds = score_grad(h)
            p_high, p_low = halves(p)
            dv_t = dv_t + nt(g, p_high) + nt(g, p_low)
            dk_rot = dk_rot + precise(nt, q_rot[h], ds)
            probs[h] = ds
        dk_t = unrot(dk_rot, angles[0], angles[1])
        dks[...] = jnp.concatenate(
            [dk_t.reshape(16, 8, TOK), dv_t.reshape(16, 8, TOK)], axis=1
        ).astype(BF)
        dk_start()
        dkr[me] = dks[me]

    task("bwd", backward)

    def query_grad():
        for h in range(2):
            dq = unrot(precise(nn, k_rot[...], probs[h]), angles[0], angles[1])
            dq_own[pl.ds(h * HD, HD), :] = dq.astype(BF)
        push(dq_own, dq_far, cp_s.at[3], cp_r.at[3], dp=cpart)

    task("bwq", query_grad)

    def key_grad():
        dk_wait()
        by_column = jnp.where(natural(i0) == i1, 1.0, 0.0).astype(BF)
        dkv = jnp.sum(dkr[...].astype(F32).reshape(4, 4, 16, TOK), axis=1).reshape(64, TOK)
        dk_own[...] = nn(by_column, dkv.astype(BF)).astype(BF)
        push(dk_own, dk_far, cp_s.at[4], cp_r.at[4], dp=cpart)

    task("dkfin", key_grad)

    def down(d, k, g):
        zs, ys, r = block(d, k, -g)
        term = (nn(wq[r, :], dq_own[...]) + nn(wkv[r, :], dk_own[...])).astype(BF)
        pd[zs, ys] = term
        high, low = halves(toks[zs, ys].astype(F32) * gain_of(zs * 2 + ys))
        projected[...] += nn(high, term) + nn(low, term)

    for d, k, g in SLOTS:
        task(name("proj", d, k, g), call(project, d, k, g))
        task(name("clipo", d, k, g), call(cast_out, d, k, g))
        task(name("back", d, k, g), call(back, d, k, g))
        task(name("mix", d, k, g), call(mix, d, k, g))
        task(name("down", d, k, g), call(down, d, k, g))

    def send_product():
        diagonal = lax.broadcasted_iota(jnp.int32, (TOK, TOK), 0) == lax.broadcasted_iota(
            jnp.int32, (TOK, TOK), 1
        )
        own = jnp.sum(jnp.where(diagonal, projected[...], 0.0), axis=0, keepdims=True)
        pr[me] = jnp.broadcast_to(own, (8, TOK))
        pr_start()

    task("prx", send_product)

    def scatter(q, p, r0, r1, y, ss, rs):
        rows_n = p.shape[2]
        half = rows_n // 2

        def cut(sign):
            return pl.ds(0 if sign > 0 else half, half)

        whole = pl.ds(0, rows_n)

        def place(d, k, sign):
            return spot(z + sign * d, k)

        def side_area(d, sign):
            return cut(-sign) if d == 2 else whole

        def side_slot(d, sign):
            return {4: 0, 3: 1, 2: 3, 0: 5}[d] + (1 if sign < 0 else 0)

        def send_side(d, sign=1):
            zs, ys = place(d, 1, sign)
            a, i = side_area(d, sign), side_slot(d, sign)
            push(p.at[zs, ys, a], y.at[i, a], ss.at[i], rs.at[i], tensor=ypart)

        def side(d, sign=1):
            a, i = side_area(d, sign), side_slot(d, sign)
            v = y.at[i, a]
            copy(v, v, ss.at[i], rs.at[i], tensor=ypart).wait_recv()
            return y[i, a].astype(F32)

        def add(zs, ys, a, *terms):
            total = p[zs, ys, a].astype(F32)
            for t in terms:
                total = total + t
            p[zs, ys, a] = total.astype(BF)

        def ends(st, k, sign):
            j = 0 if sign > 0 else 1
            to = r0.at[j, st - 1] if k == 0 else r1.at[j, st - 3]
            i = 6 + (st - 1) * 2 + j if k == 0 else 14 + (st - 3) * 2 + j
            return (to.at[cut(sign)] if st == 1 or (st == 3 and k == 1) else to), i

        def send(st, k, sign):
            zs, ys = place(5 - st, k, sign)
            v = p.at[zs, ys]
            if st == 1 or (st == 3 and k == 1):
                v = p.at[zs, ys, cut(sign)]
            to, i = ends(st, k, sign)
            push(v, to, ss.at[i], rs.at[i], tensor=zdev(sign))

        def wait(st, k, sign):
            v, i = ends(st, k, sign)
            copy(v, v, ss.at[i], rs.at[i], tensor=zdev(sign)).wait_recv()
            return v[...].astype(F32)

        def first():
            zs, ys = place(4, 0, 1)
            add(zs, ys, whole, side(4))
            for sign in DIRS:
                send(1, 0, sign)

        def step(st, sign):
            zs, ys = place(4 - st, 0, sign)
            if st == 1:
                add(zs, ys, whole, side(3, sign))
                add(zs, ys, cut(sign), wait(1, 0, sign))
            elif st == 2:
                add(zs, ys, cut(-sign), side(2, sign))
                add(zs, ys, whole, wait(2, 0, sign))
            else:
                add(zs, ys, whole, wait(3, 0, sign))
            send(st + 1, 0, sign)

        def near(sign):
            zs, ys = place(1, 1, sign)
            add(zs, ys, cut(sign), wait(3, 1, sign))
            send(4, 1, sign)

        def total(k):
            zs, ys = spot(z, k)
            return p[zs, ys].astype(F32) + (wait(4, k, 1) + wait(4, k, -1))

        def cross():
            p[z, 1 - yh] = total(1).astype(BF)
            send_side(0)

        def finish():
            return total(0) + side(0)

        task(q + "side4", call(send_side, 4))
        task(q + "first", first)
        task(q + "cross", cross)
        for g in DIRS:
            task(name(q + "side3,", g), call(send_side, 3, g))
            task(name(q + "side2,", g), call(send, 3, 1, g), call(send_side, 2, g))
            task(name(q + "near,", g), call(near, g))
            for st in (1, 2, 3):
                task(name(q + "step", st, g), call(step, st, g))
        return finish

    def group_sum(q, make, p, r, y, ss, rs):
        rows_n = p.shape[1]
        half = rows_n // 2

        def where(xx, k):
            return lax.rem(xx + NX, NX) * 2 + (yl if k == 0 else 1 - yl)

        def number(st, k, sign):
            return (st - 1) * 4 + k * 2 + (0 if sign > 0 else 1)

        def ends(st, k, sign):
            to = r.at[0 if sign > 0 else 1, st - 1, k]
            return to.at[pl.ds(0 if sign > 0 else half, half)] if st == 1 else to

        def send(st, k, sign):
            v = p.at[where(x + sign * (3 - st), k)]
            if st == 1:
                v = v.at[pl.ds(0 if sign > 0 else half, half)]
            i = number(st, k, sign)
            push(v, ends(st, k, sign), ss.at[i], rs.at[i], dp=xdev(sign))

        def wait(st, k, sign):
            v = ends(st, k, sign)
            i = number(st, k, sign)
            copy(v, v, ss.at[i], rs.at[i], dp=xdev(sign)).wait_recv()

        def step(k, sign):
            wait(1, k, sign)
            s = where(x + sign, k)
            a = pl.ds(0 if sign > 0 else half, half)
            j = 0 if sign > 0 else 1
            p[s, a] = (p[s, a].astype(F32) + r[j, 0, k, a].astype(F32)).astype(BF)
            send(2, k, sign)

        def total(k):
            for sign in DIRS:
                wait(2, k, sign)
            return p[where(x, k)].astype(F32) + (r[0, 1, k].astype(F32) + r[1, 1, k].astype(F32))

        def cross():
            p[where(x, 1)] = total(1).astype(BF)
            push(p.at[where(x, 1)], y, ss.at[8], rs.at[8], dp=ylpart)

        def finish():
            own = total(0)
            copy(y, y, ss.at[8], rs.at[8], dp=ylpart).wait_recv()
            return own + y[...].astype(F32)

        def start(k):
            for g in DIRS:
                send(1, k, g)

        for k in (0, 1):
            for dx in (2, 1, -1, 0):
                task(q + "g%d,%d" % (dx, k), call(lambda dx, k: make(where(x + dx, k)), dx, k))
            task(q + "send1,%d" % k, call(start, k))
            for g in DIRS:
                task(name(q + "step,", k, g), call(step, k, g))
        task(q + "cross", cross)
        return finish

    m_finish = scatter("M", pm, rm0, rm1, ym, zm_s, zm_r)
    n_finish = scatter("N", pd, rd0, rd1, yd, zd_s, zd_r)

    waited = set()

    def once(key, src, dst, i):
        if key not in waited:
            waited.add(key)
            copy(src, dst, cp_s.at[i], cp_r.at[i], dp=cpart).wait_recv()

    def out_grads(s):
        once("gout", pgout, pgout, 2)
        once("att", att_far, att_far, 1)
        sgo[s] = (nn(att_own[...], gout[s, core]) + nn(att_far[...], pgout[s])).astype(BF)

    def query_grads(s):
        once("acts", pacts, pacts, 0)
        once("dq", dq_far, dq_far, 3)
        sgw[s] = (nn(dq_own[...], acts[s, core]) + nn(dq_far[...], pacts[s])).astype(BF)

    def key_grads(s):
        once("acts", pacts, pacts, 0)
        once("dk", dk_far, dk_far, 4)
        sgv[s] = (nn(dk_own[...], acts[s, core]) + nn(dk_far[...], pacts[s])).astype(BF)

    o_finish = group_sum("O", out_grads, sgo, xgo, ygo, xo_s, xo_r)
    w_finish = group_sum("W", query_grads, sgw, xgw, ygw, xw_s, xw_r)
    v_finish = group_sum("V", key_grads, sgv, xgv, ygv, xv_s, xv_r)

    outs = []

    def emit(src, to):
        c = pltpu.make_async_copy(src, to, out_sem.at[len(outs)])
        c.start()
        outs.append(c)

    def end_mixed():
        mixed_out[0] = m_finish().astype(BF)
        emit(mixed_out, mixed_hbm)

    def end_out():
        go_out[...] = o_finish()
        emit(go_out, go_hbm)

    def end_query():
        gq_out[...] = w_finish().T
        emit(gq_out, gq_hbm)

    def end_key():
        gkv_out[...] = v_finish()
        emit(gkv_out, gkv_hbm)

    def end_down():
        scaled_rows[...] = n_finish().T * gain_of(me)

    def end_tokens():
        pr_wait()
        inv = lane_inv[:, pl.ds(0, 1)]
        proj = jnp.broadcast_to(jnp.sum(pr[...], axis=0)[:1], (128, TOK)).T[:, :1]
        slope = inv * inv * inv * proj / (FEAT * 16)
        dtok_out[0] = (inv * scaled_rows[...] - tok_ref[0].astype(F32) * slope).astype(BF)
        emit(dtok_out, dtok_hbm)

    task("Mfin", end_mixed)
    task("Ofin", end_out)
    task("Wfin", end_query)
    task("Vfin", end_key)
    task("Nfin", end_down)
    task("out", end_tokens)

    listed = list(tasks.values())
    assert sorted(ORDER) == list(range(len(listed)))
    for number in ORDER:
        for step in listed[number]:
            step()

    for c in sent:
        c.wait_send()
    mg_drain()
    kv_drain()
    dk_drain()
    pr_drain()
    for c in outs:
        c.wait()


def spread(mixed, dtok, gq, gkv, go, mixed_to, dtok_to, gq_to, gk_to, gv_to, go_to):
    mixed_to[...] = mixed[...]
    dtok_to[...] = dtok[...]
    gq_to[...] = gq[...]
    go_to[...] = go[...]
    gk_to[...] = gkv[pl.ds(0, KC), :]
    gv_to[...] = gkv[pl.ds(KC, KC), :]


def body(
    tokens, norm_gain, w_query, w_key, w_value, w_output, positions, scale_exps, loss_exp, out_grad
):
    vmem = pl.BlockSpec(memory_space=pltpu.VMEM)
    smem = pl.BlockSpec(memory_space=pltpu.SMEM)
    hbm = pl.BlockSpec(memory_space=pl.ANY)
    V = pltpu.VMEM
    dma = pltpu.SemaphoreType.DMA
    S = jax.ShapeDtypeStruct
    sums = [
        V((8, 2, TOK, FEAT), BF), V((2, 4, TOK, FEAT), BF), V((2, 2, TOK, FEAT), BF),
        V((6, TOK, FEAT), BF),
    ]
    sums_down = [
        V((8, 2, FEAT, TOK), BF), V((2, 4, FEAT, TOK), BF), V((2, 2, FEAT, TOK), BF),
        V((6, FEAT, TOK), BF),
    ]
    def by_group(n):
        return V((8, n, FEAT), BF), V((2, 2, 2, n, FEAT), BF), V((n, FEAT), BF)

    parts = pl.pallas_call(
        kernel,
        out_shape=(
            S((1, TOK, FEAT), BF), S((1, TOK, FEAT), BF), S((FEAT, QC), F32),
            S((2 * KC, FEAT), F32), S((QC, FEAT), F32),
        ),
        in_specs=[smem, smem, vmem, vmem, vmem, vmem, hbm, hbm, hbm, hbm],
        out_specs=(hbm,) * 5,
        scratch_shapes=[
            V((1, TOK, FEAT), BF), V((1, TOK, FEAT), BF), V((FEAT, QC), F32), V((QC, FEAT), F32),
            V((2 * KC, FEAT), F32),
            V((8192, QC), BF), V((KC, 8192), BF), V((KC, 8192), BF), V((8192, 2 * KC), BF),
            V((QC, 8192), BF),
            V((8, 2, TOK, FEAT), BF), V((8, 2, TOK, FEAT), BF), V((8, 2, TOK, FEAT), BF),
            V((8, TOK, FEAT), BF), V((8, TOK, FEAT), BF),
            *sums, *sums_down,
            *by_group(QC), *by_group(QC), *by_group(64),
            V((QC, TOK), BF), V((QC, TOK), BF), V((QC, TOK), BF), V((QC, TOK), BF),
            V((64, TOK), BF), V((64, TOK), BF),
            V((2, TOK, TOK), F32), V((2, HD, TOK), F32), V((HD, TOK), F32), V((TOK, HD), BF),
            V((TOK, 128), F32), V((2, 64, TOK), F32), V((TOK, TOK), F32), V((TOK, FEAT), F32),
            V((16, 8, 128), F32), V((4, 16, TOK), BF), V((16, 16, TOK), BF),
            V((16, 16, TOK), BF), V((16, 16, TOK), BF), V((16, 8, TOK), F32),
            V((TOK, QC), F32), V((TOK, 2 * KC), F32), V((QC, TOK), F32),
            dma((4,)), dma((5,)),
            dma((22,)), dma((22,)), dma((22,)), dma((22,)),
            dma((18,)), dma((18,)), dma((18,)), dma((18,)),
            dma((9,)), dma((9,)), dma((9,)), dma((9,)), dma((9,)), dma((9,)),
            dma((4, 16)), dma((4, 16)), dma((5,)), dma((5,)),
        ],
        compiler_params=pltpu.CompilerParams(
            collective_id=0, has_side_effects=True, vmem_limit_bytes=60 * 1024 * 1024
        ),
    )(
        scale_exps, loss_exp, tokens, norm_gain, positions, out_grad,
        w_query, w_key.T, w_value.T, w_output,
    )
    mixed, d_rows, grad_query, grad_key, grad_value, grad_output = pl.pallas_call(
        spread,
        out_shape=(
            S((1, TOK, FEAT), BF), S((1, TOK, FEAT), BF), S((FEAT, QC), F32),
            S((KC, FEAT), F32), S((KC, FEAT), F32), S((QC, FEAT), F32),
        ),
        in_specs=[vmem] * 5,
        out_specs=(vmem,) * 6,
    )(*parts)
    return mixed, d_rows, grad_query, grad_key.T, grad_value.T, grad_output


def solution(mesh):
    placed = (
        P("dp", None, "tensor"),
        P("tensor"),
        P(None, "tensor"),
        P(None, "tensor"),
        P(None, "tensor"),
        P("tensor", None),
        P("dp", None),
        P(),
        P(),
        P("dp", None, "tensor"),
    )
    return jax.shard_map(
        body,
        mesh=mesh,
        in_specs=placed,
        out_specs=(
            P("dp", None, "tensor"),
            P("dp", None, "tensor"),
            P("dp", "tensor"),
            P("dp", "tensor"),
            P("dp", "tensor"),
            P("tensor", "dp"),
        ),
        check_vma=False,
    )
```

time: 1390 us -> 104 us (0.07)
  waiting for transfers between devices: 1120 us -> 0 us
  blocking collectives: 161 us -> 0 us
  Pallas kernels: 0 us -> 101 us
  matrix products: 55.5 us -> 0 us
  other arithmetic: 20.3 us -> 0 us
  between operations: 19.7 us -> 1.29 us
    reduce_scatter x8 -> x0, waiting for transfers between devices: 1010 us -> none  [the longest x2 431 us: share_cols(): lax.psum_scatter(term.astype(jnp.bfloat16), 'tensor', scatter_dimension=1...]
    all_gather x2 -> x0, waiting for transfers between devices: 111 us -> none  [gather_cols(): return lax.all_gather(rows, 'tensor', axis=1, tiled=True)]
    pallas_call x0 -> x2, Pallas kernels: none -> 101 us  [the longest x1 99 us: body(): pl.pallas_call(kernel, out_shape=(S((1, TOK, FEAT), BF), S((1, TOK, FEAT)...]
    psum x2 -> x0, blocking collectives: 84.4 us -> none  [the longest x1 45.1 us: body(): squares = lax.psum(jnp.sum(local_rows * local_rows, axis=1), 'tensor')]
    all_gather x2 -> x0, blocking collectives: 76.3 us -> none  [the longest x1 39.1 us: body(): lax.all_gather(value_cols, 'tensor', axis=1, tiled=True)]
    dot_general x22 -> x0, matrix products: 55.5 us -> none  [the longest x4 13.4 us: contract_cols(): lax.dot_general(left, right, (((1,), (1,)), ((), ())), preferred_element_...]
  transfers between devices with their start and end apart: 10 -> 0, of which waited for: 10 -> 0; matrix products, arithmetic and copies ran while one was open for 4% -> 0% of each run, Pallas kernels for 0% -> 0%
where the time goes in v2:
time: 104 us; the launch traced here: 103 us
  Pallas kernels  101 us (97%)
  between operations  1.29 us (1%)
    pallas_call x1, Pallas kernels, body(): pl.pallas_call(kernel, out_shape=(S((1, TOK, FEAT), BF), S((1, TOK, FEAT)...  99 us
    pallas_call x1, Pallas kernels, body(): pl.pallas_call(spread, out_shape=(S((1, TOK, FEAT), BF), S((1, TOK, FEAT)...  2.5 us

profile of v2, /device:TPU:6, one launch (start us, length us, event | category | flops | bytes accessed | tf_op | source)
XLA Modules:
  0.0 102.7 jit_solution(11409829644523985842)
XLA Ops:
  1.3 99.0 %shard_map.145 = (bf16[1,128,512]{2,1,0:T(8,128)(2,1)}, bf16[1,128,512]{2,1,0:T(8,128)(2,1)}, f32[512,256]{1,0:T(8,128)}, f32[64,512]{1,0:T(8,128)}, f32[256,512]{1,0:T(8,128)}) custom-call(s32[7]{0:T(128)} %scale_ref.1, s32[1]{0:T(128)S(6)} %copy.16.loss_ref, bf16[1,128,512]{2,1,0:T(8,128)(2,1)} %tok_ref.1, bf16[512]{0:T(512)(128)(2,1)} %gain_ref.1, ...), custom_call_target="tpu_custom_call" | custom-call | tf_op jit(solution)/shard_map/pallas_call | solution.py:714
  100.2 2.5 %shard_map.146 = (bf16[1,128,512]{2,1,0:T(8,128)(2,1)}, bf16[1,128,512]{2,1,0:T(8,128)(2,1)}, f32[512,256]{1,0:T(8,128)}, f32[32,512]{1,0:T(8,128)}, f32[32,512]{1,0:T(8,128)}, /*index=5*/f32[256,512]{1,0:T(8,128)}) custom-call(bf16[1,128,512]{2,1,0:T(8,128)(2,1)} %get-tuple-element.17.mixed, bf16[1,128,512]{2,1,0:T(8,128)(2,1)} %get-tuple-element.18.dtok, ...), custom_call_target="tpu_custom_call" | custom-call | tf_op jit(solution)/shard_map/pallas_call | solution.py:751

commit v3 on v2

--- a/solution.py
+++ b/solution.py
@@ -57,32 +57,32 @@
 
 
 ORDER = (
-    0, 16, 32, 2, 9, 1, 33, 78, 108, 58, 113, 98, 68, 73, 93, 48, 43, 118, 83, 63, 44, 88, 53, 103,
-    52, 3, 10, 13, 62, 47, 6, 57, 82, 42, 18, 25, 17, 49, 84, 54, 12, 92, 5, 87, 4, 7, 67, 11, 72,
-    14, 19, 26, 64, 59, 22, 29, 21, 28, 94, 89, 97, 102, 107, 8, 15, 77, 112, 20, 27, 23, 69, 30,
-    74, 99, 104, 117, 34, 24, 35, 31, 79, 38, 109, 114, 119, 37, 36, 80, 120, 123, 39, 115, 132,
-    75, 110, 126, 160, 164, 70, 100, 127, 105, 133, 40, 65, 60, 155, 90, 161, 153, 157, 95, 162,
-    156, 124, 163, 154, 55, 171, 177, 175, 179, 128, 45, 134, 85, 169, 166, 165, 50, 41, 121, 138,
-    81, 116, 51, 147, 111, 141, 135, 76, 129, 159, 158, 91, 106, 148, 71, 46, 86, 66, 56, 96, 61,
-    101, 142, 125, 122, 183, 187, 181, 185, 186, 139, 136, 192, 193, 130, 191, 178, 170, 149, 176,
-    143, 180, 167, 168, 184, 190, 194, 172, 150, 144, 131, 137, 188, 189, 140, 199, 151, 145, 182,
-    196, 195, 198, 174, 173, 152, 146, 197, 201, 202, 203, 200,
+    0, 46, 3, 13, 1, 5, 15, 2, 4, 14, 19, 47, 8, 116, 76, 126, 131, 96, 106, 56, 101, 111, 6, 16,
+    23, 61, 66, 86, 121, 71, 91, 81, 57, 18, 9, 60, 75, 100, 7, 10, 21, 70, 105, 55, 65, 17, 20,
+    85, 11, 80, 36, 24, 95, 26, 25, 38, 97, 67, 28, 62, 110, 115, 12, 22, 90, 31, 37, 42, 27, 125,
+    102, 120, 41, 107, 29, 72, 32, 39, 77, 130, 44, 48, 30, 33, 49, 117, 34, 82, 40, 112, 87, 43,
+    35, 45, 92, 122, 50, 127, 108, 133, 138, 123, 113, 140, 98, 103, 73, 78, 88, 63, 118, 151, 83,
+    68, 58, 93, 128, 132, 52, 53, 51, 152, 142, 139, 141, 150, 143, 154, 153, 136, 193, 186, 194,
+    195, 188, 187, 196, 189, 54, 134, 163, 124, 129, 94, 114, 119, 175, 164, 176, 165, 89, 84, 109,
+    104, 177, 79, 74, 197, 166, 99, 69, 64, 59, 147, 158, 135, 168, 203, 178, 167, 190, 137, 179,
+    155, 144, 201, 204, 198, 199, 148, 180, 159, 202, 169, 162, 208, 161, 183, 172, 192, 191, 145,
+    156, 149, 181, 170, 160, 207, 173, 184, 200, 146, 157, 182, 171, 174, 185, 205, 206, 209, 210,
 )
 
 
 def kernel(
-    scale_ref, loss_ref, tok_ref, gain_ref, pos_ref, og_ref, wq_hbm, wk_hbm, wv_hbm, wo_hbm,
+    scale_ref, loss_ref, tok_hbm, gain_hbm, pos_hbm, og_hbm, wq_hbm, wk_hbm, wv_hbm, wo_hbm,
     mixed_hbm, dtok_hbm, gq_hbm, gkv_hbm, go_hbm,
     mixed_out, dtok_out, gq_out, go_out, gkv_out,
-    wq, wkt, wvt, wkv, wo, toks, acts, gout, pacts, pgout,
-    pm, rm0, rm1, ym, pd, rd0, rd1, yd,
-    sgo, xgo, ygo, sgw, xgw, ygw, sgv, xgv, ygv,
-    att_own, att_far, dq_own, dq_far, dk_own, dk_far, probs, q_rot, k_rot, v_rows, lane_inv,
-    angles, projected, scaled_rows,
+    wq, wkt, wvt, wkv, wo, toks, acts, gout, pgout,
+    pm, rm, pd, rd,
+    sgo, xgo, ygo, actr, dqr, dkr_all, w_send, w_own, w_far, v_send, v_own, v_far,
+    att_own, att_far, dq_own, dk_own, probs, q_rot, k_rot, v_rows, lane_inv,
+    angles, projected, scaled_rows, gain_ref, pos_ref,
     mg, kvs, kvr, dks, dkr, pr,
     qacc, kvacc, dacc,
     load_sem, out_sem, gt_s, gt_r, gg_s, gg_r, zm_s, zm_r, zd_s, zd_r, xo_s, xo_r,
-    xw_s, xw_r, xv_s, xv_r, sm_s, sm_r, cp_s, cp_r,
+    aa_s, aa_r, dq_s, dq_r, dk_s, dk_r, sm_s, sm_r, cp_s, cp_r,
 ):
     dp = lax.axis_index("dp")
     me = lax.axis_index("tensor")
@@ -123,12 +123,27 @@
     ylpart = x * 4 + (1 - yl) * 2 + core
     cpart = x * 4 + yl * 2 + (1 - core)
 
+    def near(n, sign):
+        return lax.rem(x + sign * (n // 2) + NX, NX), (core if n % 2 == 0 else 1 - core)
+
+    def near_dp(n, sign):
+        xs, cs = near(n, sign)
+        return xs * 4 + yl * 2 + cs
+
+    first_load = pltpu.make_async_copy(tok_hbm.at[0], toks.at[z, yh], load_sem.at[4])
+    first_load.start()
     loads = [
         pltpu.make_async_copy(wk_hbm, wkt, load_sem.at[0]),
         pltpu.make_async_copy(wv_hbm, wvt, load_sem.at[1]),
         pltpu.make_async_copy(wq_hbm, wq, load_sem.at[2]),
         pltpu.make_async_copy(wo_hbm, wo, load_sem.at[3]),
     ]
+    grad_load = pltpu.make_async_copy(og_hbm.at[0], gout.at[z, yh], load_sem.at[5])
+    gain_load = pltpu.make_async_copy(gain_hbm, gain_ref, load_sem.at[6])
+    pos_load = pltpu.make_async_copy(pos_hbm, pos_ref, load_sem.at[7])
+    grad_load.start()
+    gain_load.start()
+    pos_load.start()
     for c in loads:
         c.start()
 
@@ -141,33 +156,17 @@
         return carry
 
     lax.fori_loop(1, 16, greet, 0)
-    for other in (xdev(1), xdev(-1), ylpart, cpart):
+    for other in [near_dp(n, 1) for n in range(1, 8)] + [ylpart]:
         pl.semaphore_signal(barrier, inc=1, device_id={"dp": other}, device_id_type=MESH)
 
     lims = [E4_TOP * power_of_half(scale_ref[i]) for i in range(6)]
     glim = E5_TOP * power_of_half(scale_ref[6] + loss_ref[0])
 
-    toks[z, yh] = tok_ref[0]
-    gout[z, yh] = clip(og_ref[0].astype(F32), glim).astype(BF)
-    rows = tok_ref[0].astype(F32)
-    gain = gain_ref[...].astype(F32).reshape(1, FEAT)
-
     def as_row(column):
         return jnp.broadcast_to(column, (TOK, 128)).T
 
-    lanes = [gain[:, i * 128 : (i + 1) * 128] for i in range(4)]
-    squares_own = as_row(jnp.sum(rows * rows, axis=1, keepdims=True))[:4]
-    mg[me] = jnp.concatenate(lanes + [squares_own], axis=0)
-    pos = pos_ref[...]
-    pair = lax.broadcasted_iota(jnp.int32, (64, TOK), 0).astype(F32)
-    angle = pos.astype(F32) * jnp.exp(pair * (-2.0 * math.log(500000.0) / HD))
-    angles[0] = jnp.cos(angle)
-    angles[1] = jnp.sin(angle)
-    qacc[...] = jnp.zeros_like(qacc)
-    kvacc[...] = jnp.zeros_like(kvacc)
-    dacc[...] = jnp.zeros_like(dacc)
-    projected[...] = jnp.zeros_like(projected)
-    pl.semaphore_wait(barrier, 19)
+    first_load.wait()
+    pl.semaphore_wait(barrier, 23)
 
     def spot(zz, k):
         return lax.rem(zz + NZ, NZ), (yh if k == 0 else 1 - yh)
@@ -175,64 +174,83 @@
     def half_of(sign):
         return pl.ds(0 if sign > 0 else TOK // 2, TOK // 2)
 
-    def gather(p, buf, ss, rs):
-        def view(zz, k, part=None):
+    def gather(p, buf, ss, rs, prepare=None):
+        def part(zz, k, h):
             zs, ys = spot(zz, k)
-            return buf.at[zs, ys] if part is None else buf.at[zs, ys, half_of(part)]
-
-        def ring(d, k, sign, zz):
-            cut = sign if (d == 4 or (d == 2 and k == 1)) else None
-            i = (d - 1) * 2 + (0 if sign > 0 else 1) + 8 * k
-            return view(zz, k, cut), i
-
-        def send(d, k, sign):
-            v, i = ring(d, k, sign, z - sign * (d - 1))
-            push(v, v, ss.at[i], rs.at[i], tensor=zdev(sign))
-
-        def wait(d, k, sign):
-            v, i = ring(d, k, sign, z - sign * d)
-            copy(v, v, ss.at[i], rs.at[i], tensor=zdev(sign)).wait_recv()
-
-        def side(d, k, sign):
-            i = 12 + d * 2 + (0 if sign > 0 else 1)
-            cut = {0: None, 2: -sign, 3: None, 4: sign}[d]
-            return view(z - sign * d, k, cut), i
-
-        def send_side(d, sign):
-            v, i = side(d, 0, sign)
+            return buf.at[zs, ys, pl.ds(h * 64, 64)]
+
+        def carried(g):
+            return 0 if g > 0 else 1
+
+        first = {(1, 0): 0, (2, 0): 4, (3, 0): 8, (4, 0): 12, (1, 1): 14, (2, 1): 18}
+
+        def ring(d, k, g, h):
+            i = first[d, k] + (0 if g > 0 else 1)
+            return i if (d, k) in ((4, 0), (2, 1)) else i + 2 * h
+
+        def send(d, k, g, h):
+            v, i = part(z - g * (d - 1), k, h), ring(d, k, g, h)
+            push(v, v, ss.at[i], rs.at[i], tensor=zdev(g))
+
+        def wait(d, k, g, h):
+            v, i = part(z - g * d, k, h), ring(d, k, g, h)
+            copy(v, v, ss.at[i], rs.at[i], tensor=zdev(g)).wait_recv()
+
+        def side(d, g, h):
+            if d == 0:
+                return 20 + h
+            return {2: 22, 3: 24, 4: 28}[d] + (0 if g > 0 else 1) + (2 * h if d == 3 else 0)
+
+        def send_side(d, g, h):
+            v, i = part(z - g * d, 0, h), side(d, g, h)
             push(v, v, ss.at[i], rs.at[i], tensor=ypart)
 
-        def wait_side(d, sign):
-            v, i = side(d, 1, sign)
+        def wait_side(d, g, h):
+            v, i = part(z - g * d, 1, h), side(d, g, h)
             copy(v, v, ss.at[i], rs.at[i], tensor=ypart).wait_recv()
 
         def begin():
-            send_side(0, 1)
+            if prepare is not None:
+                prepare()
+            for h in (0, 1):
+                send_side(0, 1, h)
+                for g in DIRS:
+                    send(1, 0, g, h)
+
+        def partner(h):
+            wait_side(0, 1, h)
             for g in DIRS:
-                send(1, 0, g)
-
-        def partner():
-            wait_side(0, 1)
-            for g in DIRS:
-                send(1, 1, g)
+                send(1, 1, g, h)
 
         task(p + "0", begin)
-        task(p + "f1,1", partner)
+        for h in (0, 1):
+            task(p + "f11%d" % h, call(partner, h))
         for g in DIRS:
-            for d, k in ((2, 0), (3, 0), (4, 0), (2, 1)):
-                task(name(p + "f", d, k, g), call(wait, d - 1, k, g), call(send, d, k, g))
-            task(name(p + "s2,", g), call(send_side, 2, g))
-            task(name(p + "s3,", g), call(send_side, 3, g))
-            task(name(p + "s4,", g), call(wait, 4, 0, g), call(send_side, 4, g))
+            n = "+" if g > 0 else "-"
+            c = carried(g)
+            for h in (0, 1):
+                task(p + "f20%s%d" % (n, h), call(wait, 1, 0, g, h), call(send, 2, 0, g, h))
+                task(p + "f30%s%d" % (n, h), call(wait, 2, 0, g, h), call(send, 3, 0, g, h))
+            task(p + "f40" + n, call(wait, 3, 0, g, c), call(send, 4, 0, g, c))
+            task(p + "f21" + n, call(wait, 1, 1, g, c), call(send, 2, 1, g, c))
+            task(p + "s2" + n, call(send_side, 2, g, 1 - c))
+            task(p + "s3%s%d" % (n, c), call(send_side, 3, g, c))
+            task(p + "s3%s%d" % (n, 1 - c), call(wait, 3, 0, g, 1 - c), call(send_side, 3, g, 1 - c))
+            task(p + "s4" + n, call(wait, 4, 0, g, c), call(send_side, 4, g, c))
 
         def arrived(d, k, g):
-            if k == 1 and d > 0:
-                if d == 1:
-                    return
-                if d == 2:
-                    wait(2, 1, g)
-                for h in DIRS if d == 4 else (g,):
-                    wait_side(d, h)
+            c = carried(g)
+            if (d, k) == (1, 1):
+                wait(1, 1, g, 1 - c)
+            elif (d, k) == (2, 1):
+                wait(2, 1, g, c)
+                wait_side(2, g, 1 - c)
+            elif (d, k) == (3, 1):
+                wait_side(3, g, 0)
+                wait_side(3, g, 1)
+            elif (d, k) == (4, 1):
+                for other in DIRS:
+                    wait_side(4, other, carried(other))
 
         return arrived
 
@@ -264,14 +282,36 @@
     pr_start, pr_wait, pr_drain = exchange(lambda peer: pr.at[me], pr, 3)
 
     t_arrived = gather("T", toks, gt_s, gt_r)
-    g_arrived = gather("G", gout, gg_s, gg_r)
-    task("mg", mg_start)
+
+    def cast_grad():
+        grad_load.wait()
+        gout[z, yh] = clip(gout[z, yh].astype(F32), glim).astype(BF)
+
+    g_arrived = gather("G", gout, gg_s, gg_r, cast_grad)
+
+    def send_squares():
+        gain_load.wait()
+        gain = gain_ref[...].astype(F32).reshape(1, FEAT)
+        lanes = [gain[:, i * 128 : (i + 1) * 128] for i in range(4)]
+        rows = toks[z, yh].astype(F32)
+        squares = as_row(jnp.sum(rows * rows, axis=1, keepdims=True))[:4]
+        mg[me] = jnp.concatenate(lanes + [squares], axis=0)
+        mg_start()
+
+    task("mg", send_squares)
 
     def gain_of(slot):
         g = mg[slot]
         return jnp.concatenate([g[i : i + 1] for i in range(4)], axis=1)
 
     def prepare():
+        pos_load.wait()
+        pair = lax.broadcasted_iota(jnp.int32, (64, TOK), 0).astype(F32)
+        angle = pos_ref[...].astype(F32) * jnp.exp(pair * (-2.0 * math.log(500000.0) / HD))
+        angles[0] = jnp.cos(angle)
+        angles[1] = jnp.sin(angle)
+        for total in (qacc, kvacc, dacc, projected):
+            total[...] = jnp.zeros_like(total)
         mg_wait()
         squares = jnp.sum(mg[...], axis=0)[4:5]
         inv_row = lax.rsqrt(squares / (FEAT * 16) + 1e-05)
@@ -284,6 +324,13 @@
     def block(d, k, g):
         zs, ys = spot(z - g * d, k)
         return zs, ys, pl.ds(pl.multiple_of((zs * 2 + ys) * 512, 512), 512)
+
+    def act_copy(zs, ys):
+        return copy(
+            acts.at[zs, ys], actr.at[x * 2 + core, lax.rem(zs, 2)],
+            aa_s.at[zs * 2 + ys], aa_r.at[(x * 2 + core) * 2 + lax.rem(zs, 2)],
+            dp=(zs // 2) * 4 + yl * 2 + ys,
+        )
 
     def project(d, k, g):
         t_arrived(d, k, g)
@@ -292,6 +339,11 @@
         a = toks[zs, ys].astype(F32) * inv * gain_of(zs * 2 + ys)
         a = clip(a, lims[0]).astype(BF)
         acts[zs, ys] = a
+
+        @pl.when(jnp.logical_or(zs // 2 != x, ys != core))
+        def _():
+            act_copy(zs, ys).start()
+
         w = clip(wq[r, :].astype(F32), lims[1]).astype(BF)
         wq[r, :] = w
         wn = jnp.concatenate(
@@ -344,7 +396,7 @@
         v_rows[...] = v_t.T.astype(BF)
         src = lax.broadcasted_iota(jnp.int32, (TOK, TOK), 0)
         dst = lax.broadcasted_iota(jnp.int32, (TOK, TOK), 1)
-        allowed = (src <= dst) & (src >= dst - pos)
+        allowed = (src <= dst) & (src >= dst - pos_ref[...])
         for h in range(2):
             score = precise(nn, k_rows, q_rot[h]) * (1.0 / math.sqrt(HD))
             weight = jnp.where(allowed, jnp.exp(jnp.where(allowed, score, 0.0)), 0.0)
@@ -364,11 +416,7 @@
     def share_gout():
         push(gout.at[:, 1 - core], pgout, cp_s.at[2], cp_r.at[2], dp=cpart)
 
-    def share_acts():
-        push(acts.at[:, 1 - core], pacts, cp_s.at[0], cp_r.at[0], dp=cpart)
-
     task("gpush", share_gout)
-    task("apush", share_acts)
 
     def score_grad(h):
         g = dacc[pl.ds(h * HD, HD), :].astype(BF)
@@ -395,11 +443,15 @@
 
     task("bwd", backward)
 
+    def to_row(src, to, ss, rs):
+        for n in range(1, 8):
+            push(src, to.at[x * 2 + core], ss.at[n], rs.at[n], dp=near_dp(n, 1))
+
     def query_grad():
         for h in range(2):
             dq = unrot(precise(nn, k_rot[...], probs[h]), angles[0], angles[1])
             dq_own[pl.ds(h * HD, HD), :] = dq.astype(BF)
-        push(dq_own, dq_far, cp_s.at[3], cp_r.at[3], dp=cpart)
+        to_row(dq_own, dqr, dq_s, dq_r)
 
     task("bwq", query_grad)
 
@@ -408,7 +460,7 @@
         by_column = jnp.where(natural(i0) == i1, 1.0, 0.0).astype(BF)
         dkv = jnp.sum(dkr[...].astype(F32).reshape(4, 4, 16, TOK), axis=1).reshape(64, TOK)
         dk_own[...] = nn(by_column, dkv.astype(BF)).astype(BF)
-        push(dk_own, dk_far, cp_s.at[4], cp_r.at[4], dp=cpart)
+        to_row(dk_own, dkr_all, dk_s, dk_r)
 
     task("dkfin", key_grad)
 
@@ -436,103 +488,96 @@
 
     task("prx", send_product)
 
-    def scatter(q, p, r0, r1, y, ss, rs):
-        rows_n = p.shape[2]
-        half = rows_n // 2
-
-        def cut(sign):
-            return pl.ds(0 if sign > 0 else half, half)
-
-        whole = pl.ds(0, rows_n)
-
-        def place(d, k, sign):
-            return spot(z + sign * d, k)
-
-        def side_area(d, sign):
-            return cut(-sign) if d == 2 else whole
-
-        def side_slot(d, sign):
-            return {4: 0, 3: 1, 2: 3, 0: 5}[d] + (1 if sign < 0 else 0)
-
-        def send_side(d, sign=1):
-            zs, ys = place(d, 1, sign)
-            a, i = side_area(d, sign), side_slot(d, sign)
-            push(p.at[zs, ys, a], y.at[i, a], ss.at[i], rs.at[i], tensor=ypart)
-
-        def side(d, sign=1):
-            a, i = side_area(d, sign), side_slot(d, sign)
-            v = y.at[i, a]
-            copy(v, v, ss.at[i], rs.at[i], tensor=ypart).wait_recv()
-            return y[i, a].astype(F32)
-
-        def add(zs, ys, a, *terms):
-            total = p[zs, ys, a].astype(F32)
+    def scatter(q, p, r, ss, rs):
+        half = p.shape[2] // 2
+        first = {(3, 1): 0, (4, 1): 2, (1, 0): 6, (2, 0): 8, (3, 0): 12, (4, 0): 16}
+
+        def area(h):
+            return pl.ds(h * half, half)
+
+        def place(d, k, g):
+            return spot(z + g * d, k)
+
+        def ring(st, k, g, h):
+            i = first[st, k] + (0 if g > 0 else 1)
+            return i if (st, k) in ((3, 1), (1, 0)) else i + 2 * h
+
+        def side(d, g, h):
+            if d in (0, 4):
+                return (28 if d == 0 else 20) + h
+            return {3: 22, 2: 26}[d] + (0 if g > 0 else 1) + (2 * h if d == 3 else 0)
+
+        def send(st, k, g, h):
+            zs, ys = place(5 - st, k, g)
+            i = ring(st, k, g, h)
+            push(p.at[zs, ys, area(h)], r.at[i], ss.at[i], rs.at[i], tensor=zdev(g))
+
+        def send_side(d, g, h):
+            zs, ys = place(d, 1, g)
+            i = side(d, g, h)
+            push(p.at[zs, ys, area(h)], r.at[i], ss.at[i], rs.at[i], tensor=ypart)
+
+        def got(st, k, g, h):
+            i = ring(st, k, g, h)
+            copy(r.at[i], r.at[i], ss.at[i], rs.at[i], tensor=zdev(g)).wait_recv()
+            return r[i].astype(F32)
+
+        def got_side(d, g, h):
+            i = side(d, g, h)
+            copy(r.at[i], r.at[i], ss.at[i], rs.at[i], tensor=ypart).wait_recv()
+            return r[i].astype(F32)
+
+        def add(d, k, g, h, *terms):
+            zs, ys = place(d, k, g)
+            total = p[zs, ys, area(h)].astype(F32)
             for t in terms:
-                total = total + t
-            p[zs, ys, a] = total.astype(BF)
-
-        def ends(st, k, sign):
-            j = 0 if sign > 0 else 1
-            to = r0.at[j, st - 1] if k == 0 else r1.at[j, st - 3]
-            i = 6 + (st - 1) * 2 + j if k == 0 else 14 + (st - 3) * 2 + j
-            return (to.at[cut(sign)] if st == 1 or (st == 3 and k == 1) else to), i
-
-        def send(st, k, sign):
-            zs, ys = place(5 - st, k, sign)
-            v = p.at[zs, ys]
-            if st == 1 or (st == 3 and k == 1):
-                v = p.at[zs, ys, cut(sign)]
-            to, i = ends(st, k, sign)
-            push(v, to, ss.at[i], rs.at[i], tensor=zdev(sign))
-
-        def wait(st, k, sign):
-            v, i = ends(st, k, sign)
-            copy(v, v, ss.at[i], rs.at[i], tensor=zdev(sign)).wait_recv()
-            return v[...].astype(F32)
-
-        def first():
-            zs, ys = place(4, 0, 1)
-            add(zs, ys, whole, side(4))
-            for sign in DIRS:
-                send(1, 0, sign)
-
-        def step(st, sign):
-            zs, ys = place(4 - st, 0, sign)
-            if st == 1:
-                add(zs, ys, whole, side(3, sign))
-                add(zs, ys, cut(sign), wait(1, 0, sign))
-            elif st == 2:
-                add(zs, ys, cut(-sign), side(2, sign))
-                add(zs, ys, whole, wait(2, 0, sign))
-            else:
-                add(zs, ys, whole, wait(3, 0, sign))
-            send(st + 1, 0, sign)
-
-        def near(sign):
-            zs, ys = place(1, 1, sign)
-            add(zs, ys, cut(sign), wait(3, 1, sign))
-            send(4, 1, sign)
-
-        def total(k):
-            zs, ys = spot(z, k)
-            return p[zs, ys].astype(F32) + (wait(4, k, 1) + wait(4, k, -1))
-
-        def cross():
-            p[z, 1 - yh] = total(1).astype(BF)
-            send_side(0)
+                total = total + t()
+            p[zs, ys, area(h)] = total.astype(BF)
+
+        def pieces(k, h):
+            return [call(got, 4, k, g, h) for g in DIRS]
+
+        for h in (0, 1):
+            task(q + "cross%d" % h, call(add, 0, 1, 1, h, *pieces(1, h)), call(send_side, 0, 1, h))
+        task(q + "side4", call(send_side, 4, 1, 0), call(send_side, 4, 1, 1))
+        for g in DIRS:
+            n = "+" if g > 0 else "-"
+            c = 0 if g > 0 else 1
+            o = 1 - c
+            task(q + "side3" + n, call(send_side, 3, g, c), call(send_side, 3, g, o))
+            task(q + "side2" + n, call(send, 3, 1, g, c), call(send_side, 2, g, o))
+            task(q + "near%s%d" % (n, o), call(send, 4, 1, g, o))
+            task(
+                q + "near%s%d" % (n, c),
+                call(add, 1, 1, g, c, call(got, 3, 1, g, c)), call(send, 4, 1, g, c),
+            )
+            task(
+                q + "first" + n,
+                call(add, 4, 0, g, c, call(got_side, 4, 1, c)), call(send, 1, 0, g, c),
+            )
+            for h in (0, 1):
+                terms = [call(got_side, 3, g, h)] + ([call(got, 1, 0, g, h)] if h == c else [])
+                task(
+                    q + "step1%s%d" % (n, h), call(add, 3, 0, g, h, *terms), call(send, 2, 0, g, h)
+                )
+                terms = [call(got, 2, 0, g, h)] + ([call(got_side, 2, g, h)] if h == o else [])
+                task(
+                    q + "step2%s%d" % (n, h), call(add, 2, 0, g, h, *terms), call(send, 3, 0, g, h)
+                )
+                task(
+                    q + "step3%s%d" % (n, h),
+                    call(add, 1, 0, g, h, call(got, 3, 0, g, h)), call(send, 4, 0, g, h),
+                )
 
         def finish():
-            return total(0) + side(0)
-
-        task(q + "side4", call(send_side, 4))
-        task(q + "first", first)
-        task(q + "cross", cross)
-        for g in DIRS:
-            task(name(q + "side3,", g), call(send_side, 3, g))
-            task(name(q + "side2,", g), call(send, 3, 1, g), call(send_side, 2, g))
-            task(name(q + "near,", g), call(near, g))
-            for st in (1, 2, 3):
-                task(name(q + "step", st, g), call(step, st, g))
+            total = []
+            for h in (0, 1):
+                t = p[z, yh, area(h)].astype(F32)
+                for piece in pieces(0, h) + [call(got_side, 0, 1, h)]:
+                    t = t + piece()
+                total.append(t)
+            return jnp.concatenate(total, axis=0)
+
         return finish
 
     def group_sum(q, make, p, r, y, ss, rs):
@@ -596,8 +641,8 @@
         task(q + "cross", cross)
         return finish
 
-    m_finish = scatter("M", pm, rm0, rm1, ym, zm_s, zm_r)
-    n_finish = scatter("N", pd, rd0, rd1, yd, zd_s, zd_r)
+    m_finish = scatter("M", pm, rm, zm_s, zm_r)
+    n_finish = scatter("N", pd, rd, zd_s, zd_r)
 
     waited = set()
 
@@ -611,19 +656,47 @@
         once("att", att_far, att_far, 1)
         sgo[s] = (nn(att_own[...], gout[s, core]) + nn(att_far[...], pgout[s])).astype(BF)
 
-    def query_grads(s):
-        once("acts", pacts, pacts, 0)
-        once("dq", dq_far, dq_far, 3)
-        sgw[s] = (nn(dq_own[...], acts[s, core]) + nn(dq_far[...], pacts[s])).astype(BF)
-
-    def key_grads(s):
-        once("acts", pacts, pacts, 0)
-        once("dk", dk_far, dk_far, 4)
-        sgv[s] = (nn(dk_own[...], acts[s, core]) + nn(dk_far[...], pacts[s])).astype(BF)
+    def act_wait():
+        if "acts" not in waited:
+            waited.add("acts")
+            for n in range(1, 8):
+                xs, cs = near(n, -1)
+                for side in (0, 1):
+                    v = actr.at[xs * 2 + cs, side]
+                    i = (xs * 2 + cs) * 2 + side
+                    copy(v, v, aa_s.at[n], aa_r.at[i], dp=near_dp(n, -1)).wait_recv()
+
+    def row_sum(q, own, to, ss, rs, out, keep, far, i):
+        def product(side):
+            act_wait()
+            total = nn(own[...], acts[x * 2 + side, core])
+            for n in range(1, 8):
+                xs, cs = near(n, -1)
+                v = to.at[xs * 2 + cs]
+                if (q, n) not in waited:
+                    waited.add((q, n))
+                    copy(v, v, ss.at[n], rs.at[n], dp=near_dp(n, -1)).wait_recv()
+                total = total + nn(to[xs * 2 + cs], actr[xs * 2 + cs, side])
+            return total
+
+        def give():
+            out[...] = product(1 - yl).astype(BF)
+            push(out, far, cp_s.at[i], cp_r.at[i], dp=ylpart)
+
+        def hold():
+            keep[...] = product(yl)
+
+        def finish():
+            copy(far, far, cp_s.at[i], cp_r.at[i], dp=ylpart).wait_recv()
+            return keep[...] + far[...].astype(F32)
+
+        task(q + "1", give)
+        task(q + "0", hold)
+        return finish
 
     o_finish = group_sum("O", out_grads, sgo, xgo, ygo, xo_s, xo_r)
-    w_finish = group_sum("W", query_grads, sgw, xgw, ygw, xw_s, xw_r)
-    v_finish = group_sum("V", key_grads, sgv, xgv, ygv, xv_s, xv_r)
+    w_finish = row_sum("W", dq_own, dqr, dq_s, dq_r, w_send, w_own, w_far, 3)
+    v_finish = row_sum("V", dk_own, dkr_all, dk_s, dk_r, v_send, v_own, v_far, 4)
 
     outs = []
 
@@ -656,7 +729,7 @@
         inv = lane_inv[:, pl.ds(0, 1)]
         proj = jnp.broadcast_to(jnp.sum(pr[...], axis=0)[:1], (128, TOK)).T[:, :1]
         slope = inv * inv * inv * proj / (FEAT * 16)
-        dtok_out[0] = (inv * scaled_rows[...] - tok_ref[0].astype(F32) * slope).astype(BF)
+        dtok_out[0] = (inv * scaled_rows[...] - toks[z, yh].astype(F32) * slope).astype(BF)
         emit(dtok_out, dtok_hbm)
 
     task("Mfin", end_mixed)
@@ -666,17 +739,37 @@
     task("Nfin", end_down)
     task("out", end_tokens)
 
+    def act_drain(slot, carry):
+        @pl.when(jnp.logical_or(slot // 4 != x, lax.rem(slot, 2) != core))
+        def _():
+            act_copy(slot // 2, lax.rem(slot, 2)).wait_send()
+
+        return carry
+
     listed = list(tasks.values())
     assert sorted(ORDER) == list(range(len(listed)))
+    names = list(tasks)
+    idle = {"att", "dkfin", "Nfin"} | {key for key in names if key.startswith(("Nstep", "Ncross"))}
+    begun = []
     for number in ORDER:
+        if names[number] in idle:
+            while begun and len(sent) - begun[0] > 24:
+                sent_first = begun.pop(0)
+                sent[sent_first].wait_send()
+        if names[number] == "att":
+            mg_drain()
+        if names[number] == "dkfin":
+            kv_drain()
+            lax.fori_loop(0, 16, act_drain, 0)
+        if names[number] == "Nfin":
+            dk_drain()
+        before = len(sent)
         for step in listed[number]:
             step()
-
-    for c in sent:
-        c.wait_send()
-    mg_drain()
-    kv_drain()
-    dk_drain()
+        begun.extend(range(before, len(sent)))
+
+    for i in begun:
+        sent[i].wait_send()
     pr_drain()
     for c in outs:
         c.wait()
@@ -700,14 +793,9 @@
     V = pltpu.VMEM
     dma = pltpu.SemaphoreType.DMA
     S = jax.ShapeDtypeStruct
-    sums = [
-        V((8, 2, TOK, FEAT), BF), V((2, 4, TOK, FEAT), BF), V((2, 2, TOK, FEAT), BF),
-        V((6, TOK, FEAT), BF),
-    ]
-    sums_down = [
-        V((8, 2, FEAT, TOK), BF), V((2, 4, FEAT, TOK), BF), V((2, 2, FEAT, TOK), BF),
-        V((6, FEAT, TOK), BF),
-    ]
+    sums = [V((8, 2, TOK, FEAT), BF), V((30, TOK // 2, FEAT), BF)]
+    sums_down = [V((8, 2, FEAT, TOK), BF), V((30, FEAT // 2, TOK), BF)]
+
     def by_group(n):
         return V((8, n, FEAT), BF), V((2, 2, 2, n, FEAT), BF), V((n, FEAT), BF)
 
@@ -717,7 +805,7 @@
             S((1, TOK, FEAT), BF), S((1, TOK, FEAT), BF), S((FEAT, QC), F32),
             S((2 * KC, FEAT), F32), S((QC, FEAT), F32),
         ),
-        in_specs=[smem, smem, vmem, vmem, vmem, vmem, hbm, hbm, hbm, hbm],
+        in_specs=[smem, smem] + [hbm] * 8,
         out_specs=(hbm,) * 5,
         scratch_shapes=[
             V((1, TOK, FEAT), BF), V((1, TOK, FEAT), BF), V((FEAT, QC), F32), V((QC, FEAT), F32),
@@ -725,20 +813,23 @@
             V((8192, QC), BF), V((KC, 8192), BF), V((KC, 8192), BF), V((8192, 2 * KC), BF),
             V((QC, 8192), BF),
             V((8, 2, TOK, FEAT), BF), V((8, 2, TOK, FEAT), BF), V((8, 2, TOK, FEAT), BF),
-            V((8, TOK, FEAT), BF), V((8, TOK, FEAT), BF),
+            V((8, TOK, FEAT), BF),
             *sums, *sums_down,
-            *by_group(QC), *by_group(QC), *by_group(64),
-            V((QC, TOK), BF), V((QC, TOK), BF), V((QC, TOK), BF), V((QC, TOK), BF),
-            V((64, TOK), BF), V((64, TOK), BF),
+            *by_group(QC),
+            V((8, 2, TOK, FEAT), BF), V((8, QC, TOK), BF), V((8, 64, TOK), BF),
+            V((QC, FEAT), BF), V((QC, FEAT), F32), V((QC, FEAT), BF),
+            V((64, FEAT), BF), V((64, FEAT), F32), V((64, FEAT), BF),
+            V((QC, TOK), BF), V((QC, TOK), BF), V((QC, TOK), BF), V((64, TOK), BF),
             V((2, TOK, TOK), F32), V((2, HD, TOK), F32), V((HD, TOK), F32), V((TOK, HD), BF),
             V((TOK, 128), F32), V((2, 64, TOK), F32), V((TOK, TOK), F32), V((TOK, FEAT), F32),
+            V((FEAT,), BF), V((1, TOK), jnp.int32),
             V((16, 8, 128), F32), V((4, 16, TOK), BF), V((16, 16, TOK), BF),
             V((16, 16, TOK), BF), V((16, 16, TOK), BF), V((16, 8, TOK), F32),
             V((TOK, QC), F32), V((TOK, 2 * KC), F32), V((QC, TOK), F32),
-            dma((4,)), dma((5,)),
-            dma((22,)), dma((22,)), dma((22,)), dma((22,)),
-            dma((18,)), dma((18,)), dma((18,)), dma((18,)),
-            dma((9,)), dma((9,)), dma((9,)), dma((9,)), dma((9,)), dma((9,)),
+            dma((8,)), dma((5,)),
+            dma((30,)), dma((30,)), dma((30,)), dma((30,)),
+            dma((30,)), dma((30,)), dma((30,)), dma((30,)),
+            dma((9,)), dma((9,)), dma((16,)), dma((16,)), dma((8,)), dma((8,)), dma((8,)), dma((8,)),
             dma((4, 16)), dma((4, 16)), dma((5,)), dma((5,)),
         ],
         compiler_params=pltpu.CompilerParams(

time: 104 us -> 99.9 us (0.961)
  Pallas kernels: 101 us -> 98.3 us
    pallas_call x1, Pallas kernels: 99 us -> 95.8 us  [body(): pl.pallas_call(kernel, out_shape=(S((1, TOK, FEAT), BF), S((1, TOK, FEAT)...]
where the time goes in v3:
time: 99.9 us; the launch traced here: 99.6 us
  Pallas kernels  98.3 us (98%)
  between operations  1.29 us (1%)
    pallas_call x1, Pallas kernels, body(): pl.pallas_call(kernel, out_shape=(S((1, TOK, FEAT), BF), S((1, TOK, FEAT)...  95.8 us
    pallas_call x1, Pallas kernels, body(): pl.pallas_call(spread, out_shape=(S((1, TOK, FEAT), BF), S((1, TOK, FEAT)...  2.5 us

profile of v3, /device:TPU:6, one launch (start us, length us, event | category | flops | bytes accessed | tf_op | source)
XLA Modules:
  0.0 99.6 jit_solution(6404470463276555099)
XLA Ops:
  1.3 95.8 %shard_map.145 = (bf16[1,128,512]{2,1,0:T(8,128)(2,1)}, bf16[1,128,512]{2,1,0:T(8,128)(2,1)}, f32[512,256]{1,0:T(8,128)}, f32[64,512]{1,0:T(8,128)}, f32[256,512]{1,0:T(8,128)}) custom-call(s32[7]{0:T(128)} %scale_ref.1, s32[1]{0:T(128)S(6)} %copy.16.loss_ref, bf16[1,128,512]{2,1,0:T(8,128)(2,1)} %tok_hbm.1, bf16[512]{0:T(512)(128)(2,1)} %gain_hbm.1, ...), custom_call_target="tpu_custom_call" | custom-call | tf_op jit(solution)/shard_map/pallas_call | solution.py:802
  97.1 2.5 %shard_map.146 = (bf16[1,128,512]{2,1,0:T(8,128)(2,1)}, bf16[1,128,512]{2,1,0:T(8,128)(2,1)}, f32[512,256]{1,0:T(8,128)}, f32[32,512]{1,0:T(8,128)}, f32[32,512]{1,0:T(8,128)}, /*index=5*/f32[256,512]{1,0:T(8,128)}) custom-call(bf16[1,128,512]{2,1,0:T(8,128)(2,1)} %get-tuple-element.17.mixed, bf16[1,128,512]{2,1,0:T(8,128)(2,1)} %get-tuple-element.18.dtok, ...), custom_call_target="tpu_custom_call" | custom-call | tf_op jit(solution)/shard_map/pallas_call | solution.py:842

commit v4 on v3

--- a/solution.py
+++ b/solution.py
@@ -57,16 +57,16 @@
 
 
 ORDER = (
-    0, 46, 3, 13, 1, 5, 15, 2, 4, 14, 19, 47, 8, 116, 76, 126, 131, 96, 106, 56, 101, 111, 6, 16,
-    23, 61, 66, 86, 121, 71, 91, 81, 57, 18, 9, 60, 75, 100, 7, 10, 21, 70, 105, 55, 65, 17, 20,
-    85, 11, 80, 36, 24, 95, 26, 25, 38, 97, 67, 28, 62, 110, 115, 12, 22, 90, 31, 37, 42, 27, 125,
-    102, 120, 41, 107, 29, 72, 32, 39, 77, 130, 44, 48, 30, 33, 49, 117, 34, 82, 40, 112, 87, 43,
-    35, 45, 92, 122, 50, 127, 108, 133, 138, 123, 113, 140, 98, 103, 73, 78, 88, 63, 118, 151, 83,
-    68, 58, 93, 128, 132, 52, 53, 51, 152, 142, 139, 141, 150, 143, 154, 153, 136, 193, 186, 194,
-    195, 188, 187, 196, 189, 54, 134, 163, 124, 129, 94, 114, 119, 175, 164, 176, 165, 89, 84, 109,
-    104, 177, 79, 74, 197, 166, 99, 69, 64, 59, 147, 158, 135, 168, 203, 178, 167, 190, 137, 179,
-    155, 144, 201, 204, 198, 199, 148, 180, 159, 202, 169, 162, 208, 161, 183, 172, 192, 191, 145,
-    156, 149, 181, 170, 160, 207, 173, 184, 200, 146, 157, 182, 171, 174, 185, 205, 206, 209, 210,
+    0, 46, 3, 13, 1, 15, 5, 2, 4, 14, 19, 47, 8, 131, 55, 65, 6, 16, 9, 23, 70, 75, 18, 100, 60,
+    86, 105, 7, 10, 21, 71, 121, 61, 95, 96, 76, 81, 106, 116, 17, 20, 85, 126, 91, 11, 80, 36,
+    110, 66, 101, 56, 26, 57, 111, 38, 67, 28, 62, 115, 12, 22, 90, 27, 37, 42, 125, 29, 39, 72,
+    77, 32, 120, 30, 33, 44, 130, 48, 40, 25, 24, 97, 49, 87, 34, 82, 43, 35, 45, 92, 41, 31, 102,
+    122, 107, 127, 50, 118, 108, 103, 133, 113, 98, 141, 138, 128, 152, 93, 123, 132, 117, 112, 52,
+    53, 151, 140, 51, 83, 58, 78, 63, 88, 68, 150, 139, 143, 73, 154, 153, 142, 193, 186, 194, 195,
+    188, 187, 54, 134, 163, 129, 175, 94, 124, 164, 119, 176, 114, 165, 89, 84, 109, 177, 104, 166,
+    79, 74, 197, 99, 64, 137, 136, 69, 59, 196, 158, 144, 135, 178, 167, 168, 203, 190, 204, 147,
+    179, 155, 189, 202, 198, 199, 159, 145, 201, 180, 161, 162, 208, 169, 183, 192, 172, 191, 148,
+    156, 146, 160, 181, 170, 184, 173, 200, 157, 149, 207, 182, 171, 185, 174, 205, 206, 209, 210,
 )
 
 
@@ -775,13 +775,24 @@
         c.wait()
 
 
-def spread(mixed, dtok, gq, gkv, go, mixed_to, dtok_to, gq_to, gk_to, gv_to, go_to):
-    mixed_to[...] = mixed[...]
-    dtok_to[...] = dtok[...]
-    gq_to[...] = gq[...]
-    go_to[...] = go[...]
-    gk_to[...] = gkv[pl.ds(0, KC), :]
-    gv_to[...] = gkv[pl.ds(KC, KC), :]
+def spread(*refs):
+    ins, outs, held, got, put = refs[:5], refs[5:11], refs[11:16], refs[16], refs[17]
+    reads = [pltpu.make_async_copy(a, b, got.at[i]) for i, (a, b) in enumerate(zip(ins, held))]
+    parts = [(0, held[0]), (1, held[1]), (2, held[2]), (4, held[4])]
+    parts += [(3, held[3].at[pl.ds(0, KC)]), (3, held[3].at[pl.ds(KC, KC)])]
+    places = (outs[0], outs[1], outs[2], outs[5], outs[3], outs[4])
+    for c in reads:
+        c.start()
+    writes = []
+    done = set()
+    for i, ((source, view), to) in enumerate(zip(parts, places)):
+        if source not in done:
+            done.add(source)
+            reads[source].wait()
+        writes.append(pltpu.make_async_copy(view, to, put.at[i]))
+        writes[-1].start()
+    for c in writes:
+        c.wait()
 
 
 def body(
@@ -845,8 +856,13 @@
             S((1, TOK, FEAT), BF), S((1, TOK, FEAT), BF), S((FEAT, QC), F32),
             S((KC, FEAT), F32), S((KC, FEAT), F32), S((QC, FEAT), F32),
         ),
-        in_specs=[vmem] * 5,
-        out_specs=(vmem,) * 6,
+        in_specs=[hbm] * 5,
+        out_specs=(hbm,) * 6,
+        scratch_shapes=[
+            V((1, TOK, FEAT), BF), V((1, TOK, FEAT), BF), V((FEAT, QC), F32),
+            V((2 * KC, FEAT), F32), V((QC, FEAT), F32), dma((5,)), dma((6,)),
+        ],
+        compiler_params=pltpu.CompilerParams(vmem_limit_bytes=60 * 1024 * 1024),
     )(*parts)
     return mixed, d_rows, grad_query, grad_key.T, grad_value.T, grad_output
 

time: 99.9 us -> 99.9 us (level)
  Pallas kernels: 98.3 us -> 97.2 us
where the time goes in v4:
time: 99.9 us; the launch traced here: 98.7 us
  Pallas kernels  97.2 us (97%)
  between operations  1.45 us (1%)
    pallas_call x1, Pallas kernels, body(): pl.pallas_call(kernel, out_shape=(S((1, TOK, FEAT), BF), S((1, TOK, FEAT)...  94.9 us
    pallas_call x1, Pallas kernels, body(): pl.pallas_call(spread, out_shape=(S((1, TOK, FEAT), BF), S((1, TOK, FEAT)...  2.3 us

profile of v4, /device:TPU:6, one launch (start us, length us, event | category | flops | bytes accessed | tf_op | source)
XLA Modules:
  0.0 98.7 jit_solution(13521182375794628492)
XLA Ops:
  1.3 94.9 %shard_map.145 = (bf16[1,128,512]{2,1,0:T(8,128)(2,1)}, bf16[1,128,512]{2,1,0:T(8,128)(2,1)}, f32[512,256]{1,0:T(8,128)}, f32[64,512]{1,0:T(8,128)}, f32[256,512]{1,0:T(8,128)}) custom-call(s32[7]{0:T(128)} %scale_ref.1, s32[1]{0:T(128)S(6)} %copy.16.loss_ref, bf16[1,128,512]{2,1,0:T(8,128)(2,1)} %tok_hbm.1, bf16[512]{0:T(512)(128)(2,1)} %gain_hbm.1, ...), custom_call_target="tpu_custom_call" | custom-call | tf_op jit(solution)/shard_map/pallas_call | solution.py:813
  96.2 2.3 %shard_map.146 = (bf16[1,128,512]{2,1,0:T(8,128)(2,1)}, bf16[1,128,512]{2,1,0:T(8,128)(2,1)}, f32[512,256]{1,0:T(8,128)}, f32[32,512]{1,0:T(8,128)}, f32[32,512]{1,0:T(8,128)}, /*index=5*/f32[256,512]{1,0:T(8,128)}) custom-call(bf16[1,128,512]{2,1,0:T(8,128)(2,1)} %get-tuple-element.17.refs_0_, bf16[1,128,512]{2,1,0:T(8,128)(2,1)} %get-tuple-element.18.refs_1_, ...), custom_call_target="tpu_custom_call" | custom-call | tf_op jit(solution)/shard_map/pallas_call | solution.py:853
